TPU v7x, 512 devices: a whole 4x4x16 slice. The times are simulated.
512 devices in a mesh: req: 8 (over z_lo, core), ctx: 16 (over x, z_hi), tp: 4 (over y).
Axes of the slice: x: 4, y: 4, z: 16 (z_hi: 4, z_lo: 4; z = z_hi * 4 + z_lo), core: 2. Of those that a mesh axis runs over, the one named last changes fastest.
Arguments:
- queries: bfloat16 [64, 256, 64, 128], P('req', 'ctx', 'tp'), may hold values from -16 to 16
- kv_pool: bfloat16 [2, 8, 768, 8, 8, 128], P(None, 'req', 'ctx', None, 'tp'), may hold values from -16 to 16
- new_kv: bfloat16 [2, 64, 256, 8, 128], P(None, 'req', 'ctx', 'tp'), may hold values from -6 to 6
- block_table: int32 [8, 16, 48], P('req', 'ctx'), may hold values from 0 to 47, each once within a row
- cached_len: int32 [8, 8], P('req'), may hold values from 1 to 768, 3840 in all within a row
- new_len: int32 [8, 8], P('req'), may hold values from 1 to 256, 1536 in all within a row
- mamba_x: bfloat16 [64, 256, 8192], P('req', 'ctx', 'tp'), may hold values from -6 to 6
- conv_state: bfloat16 [64, 3, 8192], P('req', None, 'tp'), may hold values from -6 to 6
- conv_weight: float32 [4, 8192], P(None, 'tp'), may hold values from -3 to 3
- conv_bias: float32 [8192], P('tp'), may hold values from -3 to 3
- x_proj: bfloat16 [32, 8192], P(None, 'tp'), may hold values from -0.0625 to 0.0625
- dt_raw: bfloat16 [64, 256, 8192], P('req', 'ctx', 'tp'), may hold values from -6 to 4
- a_log: float32 [16, 8192], P(None, 'tp'), may hold values from -3 to 0.5
- skip_gain: float32 [8192], P('tp'), may hold values from 0.5 to 1.5
- ssm_state: bfloat16 [64, 16, 8192], P('req', None, 'tp'), may hold values from -6 to 6
- target_group: int32 [8, 8], P('req'), may hold values from 0 to 7, as said below
Outputs:
- attended: bfloat16 [64, 256, 64, 128], P('req', 'ctx', 'tp')
- mixed: bfloat16 [64, 256, 8192], P('req', 'ctx', 'tp')
Inputs may be any that keep to these rules, and one draw needn't show every extreme that they name: `target_group`: each row names every group exactly 1 times.
All inputs are finite; a program needn't handle non-finite values.
Results may differ from a plain program's by a relative error of at most 0.013.
Values may be sent and summed in bfloat16 or wider, within the bound.
A program may use at most 128 MiB of HBM per device.

v0:
```python
import jax
import jax.numpy as jnp
from jax import lax
from jax.sharding import PartitionSpec as P


def passed_along(value, axis, steps):
    count = lax.axis_size(axis)
    leading, last = (max(0, -steps), min(count, count - steps))
    return lax.ppermute(value, axis, [(source, source + steps) for source in range(leading, last)])


def prefix(x, axis, join, neutral):
    place = lax.axis_index(axis)
    gathered = jax.tree.map(
        lambda a, kind: lax.all_gather(a.astype(kind), axis), x, (jnp.bfloat16, jnp.bfloat16)
    )
    state = jax.tree.map(lambda a, e: jnp.zeros_like(a) + jnp.asarray(e, a.dtype), x, neutral)

    def one(turn, state):
        return join(
            state,
            jax.tree.map(
                lambda a, own: lax.dynamic_index_in_dim(a, turn, 0, False).astype(own.dtype),
                gathered,
                x,
            ),
        )

    return lax.fori_loop(0, place, one, state)


def state_step(rates, state, item):
    step, into, out, value = item
    return (
        jnp.exp(step[:, None, :] * rates[None]) * state
        + (step * value)[:, None, :] * into[:, :, None]
    )


def run_scan(rates, gains, initial_state, sequence):

    def advance(state, item):
        state = state_step(rates, state, item)
        return (state, jnp.sum(item[2][:, :, None] * state, axis=1) + gains * item[3])

    final_state, outputs = lax.scan(advance, initial_state, sequence)
    return outputs.transpose(1, 0, 2)


def per_device(
    queries,
    kv_pool,
    new_kv,
    block_table,
    cached_len,
    new_len,
    mamba_x,
    conv_state,
    conv_weight,
    conv_bias,
    x_proj,
    dt_raw,
    a_log,
    skip_gain,
    ssm_state,
    target_group,
):
    token_location = lax.axis_index("ctx")
    reqs, fresh, qheads, width = queries.shape
    kvheads = new_kv.shape[3]
    groups = qheads // kvheads
    rows = fresh * groups
    qrows = (
        queries.reshape(reqs, fresh, kvheads, groups, width)
        .transpose(0, 2, 1, 3, 4)
        .reshape(reqs, kvheads, rows, width)
    )
    qpos = token_location * fresh + jnp.arange(rows, dtype=jnp.int32) // groups
    cache_local = jnp.take(kv_pool[:, 0], block_table[0, 0], axis=1)
    span = cache_local.shape[1] * cache_local.shape[2] // reqs
    cache_local = cache_local.reshape(2, reqs, span, kvheads, width)
    clen = cached_len[0]
    nlen = new_len[0]
    scale = width ** (-0.5)

    def attend(carry, keys, values, valid):
        running, total, summed = carry
        scores = (
            jnp.einsum("rgqd,rngd->rgqn", qrows, keys, preferred_element_type=jnp.float32) * scale
        )
        scores = jnp.where(valid[:, None], scores, -1e30)
        newest = jnp.maximum(running, jnp.max(scores, axis=-1))
        weight = jnp.where(valid[:, None], jnp.exp(scores - newest[..., None]), 0.0)
        factor = jnp.exp(running - newest)
        total = total * factor + jnp.sum(weight, axis=-1)
        summed = summed * factor[..., None] + jnp.einsum(
            "rgqn,rngd->rgqd",
            weight.astype(jnp.bfloat16),
            values,
            preferred_element_type=jnp.float32,
        )
        return (newest, total, summed)

    start_carry = (
        jnp.full((reqs, kvheads, rows), -1e30, jnp.float32),
        jnp.zeros((reqs, kvheads, rows), jnp.float32),
        jnp.zeros((reqs, kvheads, rows, width), jnp.float32),
    )
    piece = lax.all_gather(cache_local, "ctx", axis=2, tiled=True)
    spot = jnp.arange(piece.shape[2], dtype=jnp.int32)
    carry = attend(
        start_carry,
        piece[0],
        piece[1],
        jnp.broadcast_to((spot[None, :] < clen[:, None])[:, None, :], (reqs, rows, spot.shape[0])),
    )
    piece = lax.all_gather(new_kv, "ctx", axis=2, tiled=True)
    spot = jnp.arange(piece.shape[2], dtype=jnp.int32)
    carry = attend(
        carry,
        piece[0],
        piece[1],
        (spot[None, None, :] <= qpos[None, :, None]) & (spot[None, None, :] < nlen[:, None, None]),
    )
    running, total, summed = carry
    attention = (
        (summed / total[..., None])
        .reshape(reqs, kvheads, fresh, groups, width)
        .transpose(0, 2, 1, 3, 4)
        .reshape(reqs, fresh, qheads, width)
    )
    live = (token_location * fresh + jnp.arange(fresh, dtype=jnp.int32))[None, :] < nlen[:, None]
    attention = jnp.where(live[:, :, None, None], attention, 0.0).astype(jnp.bfloat16)
    order = jnp.argsort(target_group[0], stable=True)
    taps = conv_weight.shape[0]
    rim = passed_along(mamba_x[:, fresh - taps + 1 :, :], "ctx", 1)
    rim = jnp.where(token_location == 0, conv_state, rim)
    padded = jnp.concatenate([rim, mamba_x], axis=1).astype(jnp.float32)
    conv_sum = conv_weight[0] * padded[:, 0:fresh]
    for tap in range(1, taps):
        conv_sum = conv_sum + conv_weight[tap] * padded[:, tap : tap + fresh]
    x_conv = jax.nn.silu(conv_sum + conv_bias).astype(jnp.bfloat16)
    incomplete_mapping = jnp.einsum(
        "rtc,sc->rts", x_conv, x_proj, preferred_element_type=jnp.float32
    )
    projected = lax.psum(incomplete_mapping, "tp")
    states = a_log.shape[0]
    rates = -jnp.exp(a_log)
    channels = mamba_x.shape[2]
    in_vec = projected[..., :states]
    out_vec = projected[..., states:]
    step_size = jax.nn.softplus(dt_raw.astype(jnp.float32))
    values = x_conv.astype(jnp.float32)
    sequence = (
        step_size.transpose(1, 0, 2),
        in_vec.transpose(1, 0, 2),
        out_vec.transpose(1, 0, 2),
        values.transpose(1, 0, 2),
    )
    empty_state = jnp.zeros((reqs, states, channels), jnp.float32)
    local_state, unused = lax.scan(
        lambda state, item: (state_step(rates, state, item), None), empty_state, sequence
    )
    elapsed = jnp.sum(step_size, axis=1)

    def combine(earlier, later):
        return (
            earlier[0] + later[0],
            jnp.exp(rates[None] * later[0][:, None, :]) * earlier[1] + later[1],
        )

    before = prefix(
        (elapsed, local_state),
        "ctx",
        combine,
        (jnp.zeros_like(elapsed), jnp.zeros_like(local_state)),
    )
    initial_state = (
        jnp.exp(rates[None] * before[0][:, None, :]) * ssm_state.astype(jnp.float32) + before[1]
    )
    outputs = run_scan(rates, skip_gain, initial_state, sequence)
    mixer = jnp.where(live[:, :, None], outputs, 0.0).astype(jnp.bfloat16)
    attention_moved, mixer_moved = (
        lax.all_to_all(
            jnp.take(attention, order, axis=0), "req", split_axis=0, concat_axis=0, tiled=True
        ),
        lax.all_to_all(
            jnp.take(mixer, order, axis=0), "req", split_axis=0, concat_axis=0, tiled=True
        ),
    )
    return (attention_moved, mixer_moved)


def solution(mesh):
    in_specs = (
        P("req", "ctx", "tp", None),
        P(None, "req", "ctx", None, "tp", None),
        P(None, "req", "ctx", "tp", None),
        P("req", "ctx", None),
        P("req", None),
        P("req", None),
        P("req", "ctx", "tp"),
        P("req", None, "tp"),
        P(None, "tp"),
        P("tp"),
        P(None, "tp"),
        P("req", "ctx", "tp"),
        P(None, "tp"),
        P("tp"),
        P("req", None, "tp"),
        P("req", None),
    )
    out_specs = (P("req", "ctx", "tp", None), P("req", "ctx", "tp"))
    return jax.shard_map(
        per_device, mesh=mesh, in_specs=in_specs, out_specs=out_specs, check_vma=False
    )
```

profile of v0, /device:TPU:6, one launch (start us, length us, event | category | flops | bytes accessed | tf_op | source)
XLA Modules:
  0.0 668.1 jit_solution(3359655009770326331)
XLA Ops:
  7.3 1.7 copy.61
  9.0 1.3 copy.63
  10.3 9.1 %collective-permute-start = (bf16[8,3,2048]{2,0,1:T(8,128)(2,1)S(1)}, bf16[8,3,2048]{2,0,1:T(8,128)(2,1)}, u32[]{:S(2)}, u32[]{:S(2)}) collective-permute-start(bf16[8,3,2048]{2,0,1:T(8,128)(2,1)S(1)} %slice.70), channel_id=1, source_target_pairs={{0,4},{4,8},{8,12},{12,16},{16,20},{20,24},{24,28},{28,32},{32,36}... | collective-permute-start | bytes 294920 | tf_op jit(solution)/shard_map/ppermute | solution.py:10
  20.0 1.3 reduce.3
  21.5 1.1 copy.89
  25.1 1.6 fusion.43
  26.7 1.8 copy.65
  28.5 0.9 broadcast_select_fusion.2
  29.5 1.5 convert_bitcast_fusion
  31.3 17.8 %psum.7 = f32[8,16,32]{2,0,1:T(8,128)S(1)} all-reduce(f32[8,16,32]{2,0,1:T(8,128)S(1)} %fusion.49), channel_id=1, replica_groups=mesh['req'=8,'ctx'=16,'tp'=4] {'tp'}, use_global_device_ids=true, to_apply=%region_6.7 | all-reduce | flops 4096 | bytes 32768 | tf_op jit(solution)/shard_map/psum | solution.py:147
  49.2 22.6 %while.37 = (s32[]{:T(128)}, f32[8,16,2048]{2,1,0:T(8,128)S(1)}, f32[16,8,2048]{2,1,0:T(8,128)S(1)}, f32[16,2048]{1,0:T(8,128)S(1)}, f32[16,8,2048]{2,1,0:T(8,12...) while((s32[]{:T(128)}, f32[8,16,2048]{2,1,0:T(8,128)S(1)}, f32[16,8,2048]{2,1,0:T(8,128)S(1)}, ...), condition=%wide.region_8.9_spmd.clone, body=%wide.region_7.8_spmd.clone.sunk | while | flops 1327107 | bytes 2688627 | solution.py:162
  71.8 1.0 convert_element_type.65
  72.8 1.0 sort.17
  74.3 76.1 %all-gather = bf16[128,2048]{1,0:T(8,128)(2,1)S(1)} all-gather(bf16[8,2048]{1,0:T(8,128)(2,1)S(1)} %get-tuple-element.267), channel_id=2, replica_groups=mesh['req'=8,'ctx'=16,'tp'=4] {'ctx'}, dimensions={0}, use_global_device_ids=true | all-gather | bytes 557056 | tf_op jit(solution)/shard_map/all_gather | solution.py:16
  150.4 3.0 fusion.15
  153.4 151.5 %all-gather.6.cloned.1.call-done = bf16[2,8,768,2,128]{4,2,3,1,0:T(8,128)(2,1)} async-done(((bf16[2,8,48,2,128]{4,2,3,1,0:T(8,128)(2,1)}), bf16[2,8,768,2,128]{4,2,3,1,0:T(8,128)(2,1)}) %all-gather.6.cloned.1.call-update) | async-done | bytes 6291472 | tf_op jit(solution)/shard_map/all_gather | solution.py:110
  304.9 3.8 bitcast_reduce_fusion
  308.8 1.0 fusion.16
  309.8 2.4 fusion.4
  312.6 4.9 fusion.23
  317.5 0.9 fusion.19
  319.3 0.9 broadcast_select_fusion.1
  320.2 3.5 all-to-all-start
  323.7 207.6 %all-gather.10.cloned.1.call-done = bf16[128,16,2048]{2,1,0:T(8,128)(2,1)} async-done(((bf16[8,16,2048]{2,1,0:T(8,128)(2,1)}), bf16[128,16,2048]{2,1,0:T(8,128)(2,1)}) %all-gather.10.cloned.1.call-update) | async-done | bytes 8388624 | tf_op jit(solution)/shard_map/all_gather | solution.py:16
  531.5 20.7 %while.35 = (s32[]{:T(128)}, f32[8,2048]{1,0:T(8,128)S(1)}, f32[8,16,2048]{2,1,0:T(8,128)S(1)}, s32[]{:T(128)}, bf16[16,8,2048]{2,1,0:T(8,128)(2,1)S(1)}, /*inde...) while((s32[]{:T(128)}, f32[8,2048]{1,0:T(8,128)S(1)}, ...), condition=%wide.region_10.11_spmd, body=%wide.region_9.10_spmd.sunk | while | flops 1097733 | bytes 3080347 | solution.py:30
  531.5 1.7 convert_add_fusion.2
  533.3 1.7 convert_add_fusion.2
  535.0 1.7 convert_add_fusion.2
  536.7 1.7 convert_add_fusion.2
  538.4 1.7 convert_add_fusion.2
  540.1 1.7 convert_add_fusion.2
  541.9 1.7 convert_add_fusion.2
  543.6 1.7 convert_add_fusion.2
  545.3 1.7 convert_add_fusion.2
  547.0 1.7 convert_add_fusion.2
  548.8 1.7 convert_add_fusion.2
  550.5 1.7 convert_add_fusion.2
  552.2 1.3 multiply_add_fusion.1
  553.4 85.4 %while.36 = (s32[]{:T(128)}, f32[8,16,2048]{2,1,0:T(8,128)S(1)}, bf16[16,8,2048]{2,0,1:T(8,128)(2,1)}, f32[16,8,2048]{2,1,0:T(8,128)}, f32[16,2048]{1,0:T(8,128)...) while((s32[]{:T(128)}, f32[8,16,2048]{2,1,0:T(8,128)S(1)}, ...), condition=%wide.region_13.14_spmd, body=%wide.region_11.13_spmd.sunk | while | flops 1622018 | bytes 3058825 | solution.py:47
  553.5 0.9 bitcast_multiply_fusion.4
  556.9 1.9 dynamic_update_slice.5
  562.2 1.9 dynamic_update_slice.5
  564.1 0.9 bitcast_multiply_fusion.4
  567.6 1.9 dynamic_update_slice.5
  572.9 1.9 dynamic_update_slice.5
  574.8 0.9 bitcast_multiply_fusion.4
  578.2 1.9 dynamic_update_slice.5
  580.1 0.9 bitcast_multiply_fusion.4
  583.6 1.9 dynamic_update_slice.5
  588.9 1.9 dynamic_update_slice.5
  590.8 0.9 bitcast_multiply_fusion.4
  594.2 1.9 dynamic_update_slice.5
  596.1 0.9 bitcast_multiply_fusion.4
  599.6 1.9 dynamic_update_slice.5
  601.5 0.9 bitcast_multiply_fusion.4
  604.9 1.9 dynamic_update_slice.5
  610.2 1.9 dynamic_update_slice.5
  615.6 1.9 dynamic_update_slice.5
  620.9 1.9 dynamic_update_slice.5
  626.3 1.9 dynamic_update_slice.5
  631.6 1.9 dynamic_update_slice.5
  636.9 1.9 dynamic_update_slice.5
  638.8 1.2 fusion.37
  640.8 19.3 %all_to_all.10 = bf16[8,16,2048]{2,1,0:T(8,128)(2,1)S(1)} all-to-all(bf16[8,16,2048]{2,1,0:T(8,128)(2,1)S(1)} %broadcast_select_fusion), channel_id=1, replica_groups=mesh['req'=8,'ctx'=16,'tp'=4] {'req'}, dimensions={0} | all-to-all | bytes 1048576 | tf_op jit(solution)/shard_map/all_to_all | solution.py:188
  (255 shorter events, 78.8 us)
Async XLA Ops:
  7.2 143.2 %copy-start = (bf16[8,16,16,128]{3,2,1,0:T(8,128)(2,1)S(1)}, bf16[8,16,16,128]{3,2,1,0:T(8,128)(2,1)}, u32[]{:S(2)}) copy-start(bf16[8,16,16,128]{3,2,1,0:T(8,128)(2,1)} %param.22) | copy-start | bytes 1572868
  7.2 17.8 %copy-start.5 = (f32[16,2048]{1,0:T(8,128)S(1)}, f32[16,2048]{1,0:T(8,128)}, u32[]{:S(2)}) copy-start(f32[16,2048]{1,0:T(8,128)} %param.34) | copy-start | bytes 393220
  7.2 17.8 %copy-start.8 = (f32[4,2048]{1,0:T(4,128)S(1)}, f32[4,2048]{1,0:T(4,128)}, u32[]{:S(2)}) copy-start(f32[4,2048]{1,0:T(4,128)} %param.30) | copy-start | bytes 98308
  7.2 17.9 %copy-start.3 = (bf16[8,16,2048]{2,1,0:T(8,128)(2,1)S(1)}, bf16[8,16,2048]{2,1,0:T(8,128)(2,1)}, u32[]{:S(2)}) copy-start(bf16[8,16,2048]{2,1,0:T(8,128)(2,1)} %param.33) | copy-start | bytes 1572868
  7.2 143.2 %all-gather.8.cloned.1.call-start = ((), (), s32[]{:S(2)}) async-start(), calls=%async_computation.3 | async-start | bytes 2228224 | tf_op jit(solution)/shard_map/all_gather | solution.py:118
  8.9 296.0 %all-gather.6.cloned.1.call-start = ((), (), s32[]{:S(2)}) async-start(), calls=%async_computation.2 | async-start | bytes 6684672 | tf_op jit(solution)/shard_map/all_gather | solution.py:110
  10.3 18.2 %collective-permute-start = (bf16[8,3,2048]{2,0,1:T(8,128)(2,1)S(1)}, bf16[8,3,2048]{2,0,1:T(8,128)(2,1)}, u32[]{:S(2)}, u32[]{:S(2)}) collective-permute-start(bf16[8,3,2048]{2,0,1:T(8,128)(2,1)S(1)} %slice.70), channel_id=1, source_target_pairs={{0,4},{4,8},{8,12},{12,16},{16,20},{20,24},{24,28},{28,32},{32,36}... | collective-permute-start | bytes 294920 | tf_op jit(solution)/shard_map/ppermute | solution.py:10
  23.9 4.6 copy-start.7
  24.9 4.6 copy-start.9
  24.9 506.4 %all-gather.10.cloned.1.call-start = ((), (), s32[]{:S(2)}) async-start(), calls=%async_computation.4 | async-start | bytes 8912896 | tf_op jit(solution)/shard_map/all_gather | solution.py:16
  29.5 1.5 copy-start.6
  49.2 23.6 %copy-start.14 = (s32[1,8]{1,0:T(1,128)S(1)}, s32[1,8]{1,0:T(1,128)}, u32[]{:S(2)}) copy-start(s32[1,8]{1,0:T(1,128)} %param.37) | copy-start | bytes 100
  49.2 24.7 %copy-start.10 = (s32[1,8]{1,0:T(1,128)S(1)}, s32[1,8]{1,0:T(1,128)}, u32[]{:S(2)}) copy-start(s32[1,8]{1,0:T(1,128)} %param.27) | copy-start | bytes 100
  49.2 24.8 %copy-start.11 = (s32[1,8]{1,0:T(1,128)S(1)}, s32[1,8]{1,0:T(1,128)}, u32[]{:S(2)}) copy-start(s32[1,8]{1,0:T(1,128)} %param.26) | copy-start | bytes 100
  71.8 81.7 %copy-start.1 = (f32[16,8,2048]{2,1,0:T(8,128)}, f32[16,8,2048]{2,1,0:T(8,128)S(1)}, u32[]{:S(2)}) copy-start(f32[16,8,2048]{2,1,0:T(8,128)S(1)} %get-tuple-element.521) | copy-start | bytes 3145732
  304.9 3.8 copy-start.2
  309.8 2.8 copy-start.12
  312.6 4.9 copy-start.13
  320.2 320.5 %all-to-all-start = ((bf16[8,16,16,128]{3,2,1,0:T(8,128)(2,1)}), bf16[8,16,16,128]{3,2,1,0:T(8,128)(2,1)S(1)}, u32[]{:S(2)}, u32[]{:S(2)}) async-start(bf16[8,16,16,128]{3,2,1,0:T(8,128)(2,1)} %broadcast_select_fusion.1), calls=%async_computation | async-start | bytes 1048576 | tf_op jit(solution)/shard_map/all_to_all | solution.py:185
  531.4 22.0 %copy-start.4 = (f32[2048]{0:T(1024)S(1)}, f32[2048]{0:T(1024)}, u32[]{:S(2)}) copy-start(f32[2048]{0:T(1024)} %param.35) | copy-start | bytes 24580
Sparse Core Ops, SparseCore 0:
  11.0 115.5 all-gather.7
  130.3 174.5 all-gather.5
  308.5 222.7 all-gather.9
where the time goes:
time: 673 us; the launch traced here: 668 us
  waiting for transfers between devices  359 us (53%)
  blocking collectives  113 us (17%)
  other arithmetic  98.7 us (15%)
  local copies, waits for them, and re-layouts  55.8 us (8%)
  between operations  14.2 us (2%)
  matrix products  13 us (2%)
  starting transfers between devices  12.7 us (2%)
    all_gather x1, waiting for transfers between devices, prefix(): lax.all_gather(a.astype(kind), axis)  208 us
    all_gather x1, waiting for transfers between devices, per_device(): piece = lax.all_gather(cache_local, 'ctx', axis=2, tiled=True)  151 us
    all_gather x1, blocking collectives, prefix(): lax.all_gather(a.astype(kind), axis)  76.1 us
    dynamic_update_slice x32, local copies, waits for them, and re-layouts, run_scan(): final_state, outputs = lax.scan(advance, initial_state, sequence)  31 us
    mul x32, other arithmetic, state_step(): step * value  27.7 us
    add x12, other arithmetic, combine(): jnp.exp(rates[None] * later[0][:, None, :]) * earlier[1] + later[1]  19.9 us
    all_to_all x1, blocking collectives, per_device(): lax.all_to_all(jnp.take(mixer, order, axis=0), 'req', split_axis=0, conca...  19.3 us
    psum x1, blocking collectives, per_device(): projected = lax.psum(incomplete_mapping, 'tp')  17.8 us
  transfers between devices with their start and end apart: 5, of which 2 were waited for; matrix products, arithmetic and copies ran while one was open for 25% of the time, Pallas kernels for 0%

commit v1 on v0

v1 whole, which is shorter than its diff:
```python
import math

import jax
import jax.numpy as jnp
from jax import lax
from jax.experimental import pallas as pl
from jax.experimental.pallas import tpu as pltpu
from jax.sharding import PartitionSpec as P

MESH = pl.DeviceIdType.MESH
F32 = jnp.float32
BF16 = jnp.bfloat16
LOG2E = math.log2(math.e)
NREQ, NCTX, NTP = 8, 16, 4
R, T, C, S = 8, 16, 2048, 16
HD = 128
SPAN = 48
TILES = C // 128
Q, KV, ST, AO, PF = range(5)


def wrap(a, n):
    return lax.rem(a + n, n)


def tile_lanes(j):
    return pl.ds(pl.multiple_of(j * 128, 128), 128)


def copy_to(axis, peer, src, dst, send_sem, recv_sem):
    return pltpu.make_async_remote_copy(
        src_ref=src,
        dst_ref=dst,
        send_sem=send_sem,
        recv_sem=recv_sem,
        device_id={axis: peer},
        device_id_type=MESH,
    )


def kernel(
    qs, kvs, rs, xt, dtt, cwb, cs, xp, a2, a2o, s0, thr, nlr, meta,
    att, mix,
    qr, kvr, rr, rf, xc, xcb, dts, pp, pr, bb, cb, av, yl, yr,
    st_s, st_r, pf_s, pf_r, ao_s, ao_r, y_s, o_s, y_all, o_all,
    ctx_send, ctx_recv, rim_send, rim_recv, tp_send, tp_recv, req_send, req_recv,
):
    g, c, p = lax.axis_index("req"), lax.axis_index("ctx"), lax.axis_index("tp")

    barrier = pltpu.get_barrier_semaphore()
    for axis, me, n in (("ctx", c, NCTX), ("tp", p, NTP), ("req", g, NREQ)):

        def greet(k, carry, axis=axis, me=me, n=n):
            pl.semaphore_signal(
                barrier, inc=1, device_id={axis: wrap(me + k, n)}, device_id_type=MESH
            )
            return carry

        lax.fori_loop(1, n, greet, 0)
    pl.semaphore_wait(barrier, NCTX + NTP + NREQ - 3)

    def ctx_copy(kind, k, src, dst):
        return copy_to(
            "ctx", wrap(c + k, NCTX), src, dst, ctx_send.at[kind, k], ctx_recv.at[kind, k]
        )

    def ctx_wait_recv(kind, dst):
        def one(k, carry):
            slot = dst.at[wrap(c - k, NCTX)]
            ctx_copy(kind, k, slot, slot).wait_recv()
            return carry

        lax.fori_loop(1, NCTX, one, 0)

    def ctx_wait_send(kind, src):
        def one(k, carry):
            slot = src.at[wrap(c + k, NCTX)]
            ctx_copy(kind, k, slot, slot).wait_send()
            return carry

        lax.fori_loop(1, NCTX, one, 0)

    rim = copy_to("ctx", wrap(c + 1, NCTX), rs, rr, rim_send, rim_recv)
    rim.start()

    def send_qkv(k, carry):
        peer = wrap(c + k, NCTX)
        ctx_copy(KV, k, kvs.at[peer], kvr.at[c]).start()
        ctx_copy(Q, k, qs.at[peer], qr.at[c]).start()
        return carry

    lax.fori_loop(1, NCTX, send_qkv, 0)
    qr[c] = qs[c]
    kvr[c] = kvs[c]

    def soften(j, carry):
        lanes = tile_lanes(j)
        d = dtt[:, lanes].astype(F32)
        dts[:, lanes] = jnp.maximum(d, 0.0) + jnp.log1p(jnp.exp(-jnp.abs(d)))
        return carry

    lax.fori_loop(0, TILES, soften, 0)

    rim.wait_recv()
    first = c == 0
    for k in range(3):
        got = rr[k].astype(F32)
        for half in range(2):
            cols = slice(half * 1024, half * 1024 + 1024)
            rows = slice(k * R, k * R + R)
            rf[rows, cols] = jnp.where(first, cs[rows, cols], got[half * R : half * R + R])

    def convolve(j, carry):
        lanes = tile_lanes(j)
        padded = jnp.concatenate([rf[:, lanes], xt[:, lanes].astype(F32)], axis=0)
        total = cwb[0:1, lanes] * padded[0 : T * R]
        for k in range(1, 4):
            total = total + cwb[k : k + 1, lanes] * padded[k * R : k * R + T * R]
        total = total + cwb[4:5, lanes]
        rounded = (total / (1.0 + jnp.exp(-total))).astype(BF16)
        xcb[:, lanes] = rounded
        xc[:, lanes] = rounded.astype(F32)
        return carry

    lax.fori_loop(0, TILES, convolve, 0)

    pp[...] = jnp.dot(xcb[...], xp[...], preferred_element_type=F32)
    for k in range(1, NTP):
        copy_to("tp", wrap(p + k, NTP), pp, pr.at[k - 1], tp_send.at[k], tp_recv.at[k]).start()
    for k in range(1, NTP):
        copy_to("tp", wrap(p + k, NTP), pp, pr.at[k - 1], tp_send.at[k], tp_recv.at[k]).wait()
    pp[...] = (pp[...] + pr[0]) + (pr[1] + pr[2])

    def spread(t, carry):
        rows = pp[pl.ds(pl.multiple_of(t * R, R), R), :]
        for s in range(S):
            bb[t * S + s] = jnp.broadcast_to(rows[:, s : s + 1], (R, 128))
            cb[t * S + s] = jnp.broadcast_to(rows[:, S + s : S + s + 1], (R, 128))
        return carry

    lax.fori_loop(0, T, spread, 0)

    def scan_tile(k, carry):
        j = wrap(c + k, NCTX)
        lanes = tile_lanes(j)
        rate = [jnp.broadcast_to(a2[s : s + 1, lanes], (R, 128)) for s in range(S)]
        gain = jnp.broadcast_to(cwb[5:6, lanes], (R, 128))

        def step(t, carry):
            elapsed, state = carry[0], carry[1:]
            rows = pl.ds(pl.multiple_of(t * R, R), R)
            d, x = dts[rows, lanes], xc[rows, lanes]
            u = d * x
            parts = [gain * x, None]
            new = []
            for s in range(S):
                decay = jnp.exp2(d * rate[s])
                av[j * (T * S) + t * S + s] = decay
                h = decay * state[s] + u * bb[t * S + s]
                new.append(h)
                y = cb[t * S + s] * h
                parts[s % 2] = y if parts[s % 2] is None else parts[s % 2] + y
            yl[rows, lanes] = parts[0] + parts[1]
            return (elapsed + d, *new)

        zero = jnp.zeros((R, 128), F32)
        last = lax.fori_loop(0, T, step, (zero,) * (S + 1))
        high = last[0].astype(BF16).astype(F32)
        packed = jnp.concatenate([*last[1:], high, last[0] - high], axis=0).astype(BF16)
        st_s[j] = packed

        @pl.when(k > 0)
        def _():
            ctx_copy(ST, k, st_s.at[j], st_r.at[c]).start()

        @pl.when(k == 0)
        def _():
            st_r[c] = packed

        return carry

    lax.fori_loop(0, NCTX, scan_tile, 0)

    ctx_wait_recv(KV, kvr)
    ctx_wait_recv(Q, qr)
    own_len = meta[R]
    factor = HD**-0.5 * LOG2E

    def attend(k, carry):
        b = wrap(c // 2 + k, NCTX // 2)
        q = qr[pl.ds(2 * b, 2)].reshape(2 * T * R, HD)
        keys = kvr[:, 0:64, :].reshape(NCTX * 64, HD)
        values = kvr[:, 64:128, :].reshape(NCTX * 64, HD)
        scores = lax.dot_general(
            q, keys, (((1,), (1,)), ((), ())), preferred_element_type=F32
        )
        row = lax.broadcasted_iota(jnp.int32, (2 * T * R, 1), 0)
        when = b * (2 * T) + row // R
        scores = jnp.where(when >= thr[...], scores, -1e30)
        top = jnp.max(scores, axis=1, keepdims=True)
        weight = jnp.exp2((scores - top) * factor)
        total = jnp.sum(weight, axis=1, keepdims=True)
        out = jnp.dot(weight.astype(BF16), values, preferred_element_type=F32) / total
        out = jnp.where(when < own_len, out, 0.0).astype(BF16)
        for half in range(2):
            peer = 2 * b + half
            part = out[half * T * R : (half + 1) * T * R]
            ao_s[peer] = part

            @pl.when(peer != c)
            def _():
                ctx_copy(
                    AO, wrap(peer - c, NCTX), ao_s.at[peer], ao_r.at[c]
                ).start()

            @pl.when(peer == c)
            def _():
                ao_r[c] = part

        return carry

    lax.fori_loop(0, NCTX // 2, attend, 0)

    ctx_wait_recv(ST, st_r)

    def advance(b, state):
        pf_s[b] = state.astype(BF16)
        item = st_r[b].astype(F32)
        elapsed = item[S * R : S * R + R] + item[S * R + R :]
        return jnp.exp2(a2o[...] * jnp.concatenate([elapsed] * S, axis=0)) * state + item[: S * R]

    lax.fori_loop(0, NCTX, advance, s0[...])

    def send_prefix(k, carry):
        peer = wrap(c + k, NCTX)
        ctx_copy(PF, k, pf_s.at[peer], pf_r.at[c]).start()
        return carry

    lax.fori_loop(1, NCTX, send_prefix, 0)
    pf_r[c] = pf_s[c]

    ctx_wait_recv(AO, ao_r)

    def req_copy(kind, k, src, dst):
        return copy_to(
            "req", wrap(g + k, NREQ), src, dst, req_send.at[kind, k], req_recv.at[kind, k]
        )

    def join_heads(i, carry):
        heads = [
            ao_r[2 * i + half].astype(F32).reshape(T, R, HD) for half in range(2)
        ]
        o_all[i] = jnp.concatenate(heads, axis=1).reshape(2 * T * R, HD).astype(BF16)
        return carry

    lax.fori_loop(0, R, join_heads, 0)

    def give_attention(k, carry):
        taker = wrap(g + k, NREQ)
        i = meta[taker]
        both = o_all[i]

        @pl.when(k > 0)
        def _():
            o_s[taker] = both
            req_copy(0, k, o_s.at[taker], att.at[g]).start()

        @pl.when(k == 0)
        def _():
            att[g] = both

        return carry

    lax.fori_loop(0, NREQ, give_attention, 0)

    def finish_tile(k, carry):
        j = wrap(c - k, NCTX)
        lanes = tile_lanes(j)

        @pl.when(k > 0)
        def _():
            ctx_copy(PF, k, pf_r.at[j], pf_r.at[j]).wait_recv()

        start = pf_r[j].astype(F32)
        limit = nlr[...]

        def step(t, state):
            rows = pl.ds(pl.multiple_of(t * R, R), R)
            parts = [yl[rows, lanes], None]
            new = []
            for s in range(S):
                h = av[j * (T * S) + t * S + s] * state[s]
                new.append(h)
                y = cb[t * S + s] * h
                parts[s % 2] = y if parts[s % 2] is None else parts[s % 2] + y
            y = jnp.where(c * T + t < limit, parts[0] + parts[1], 0.0)
            yr[j, pl.ds(t, R, stride=T), :] = y
            return tuple(new)

        lax.fori_loop(0, T, step, tuple(start[s * R : s * R + R] for s in range(S)))
        return carry

    lax.fori_loop(0, NCTX, finish_tile, 0)

    def join_tiles(i, carry):
        rows = yr[:, pl.ds(pl.multiple_of(i * T, T), T), :]
        y_all[i] = jnp.concatenate([rows[j] for j in range(TILES)], axis=1).astype(BF16)
        return carry

    lax.fori_loop(0, R, join_tiles, 0)

    def give_mixed(k, carry):
        taker = wrap(g + k, NREQ)
        i = meta[taker]
        rows = y_all[i]

        @pl.when(k > 0)
        def _():
            y_s[taker] = rows
            req_copy(1, k, y_s.at[taker], mix.at[g]).start()

        @pl.when(k == 0)
        def _():
            mix[g] = rows

        return carry

    lax.fori_loop(0, NREQ, give_mixed, 0)

    rim.wait_send()
    for kind, src in ((Q, qs), (KV, kvs), (ST, st_s), (AO, ao_s), (PF, pf_s)):
        ctx_wait_send(kind, src)

    def last(k, carry):
        taker, giver = wrap(g + k, NREQ), wrap(g - k, NREQ)
        req_copy(0, k, o_s.at[taker], att.at[giver]).wait()
        req_copy(1, k, y_s.at[taker], mix.at[giver]).wait()
        return carry

    lax.fori_loop(1, NREQ, last, 0)


def per_device(
    queries,
    kv_pool,
    new_kv,
    block_table,
    cached_len,
    new_len,
    mamba_x,
    conv_state,
    conv_weight,
    conv_bias,
    x_proj,
    dt_raw,
    a_log,
    skip_gain,
    ssm_state,
    target_group,
):
    c = lax.axis_index("ctx")
    qs = queries.reshape(R, T, 2, 8, HD).transpose(0, 2, 1, 3, 4).reshape(NCTX, T * 8, HD)
    cached = jnp.take(kv_pool[:, 0], block_table[0, 0], axis=1)
    cached = cached.reshape(2, R, SPAN, 2, HD).transpose(1, 3, 0, 2, 4)
    fresh = new_kv.transpose(1, 3, 0, 2, 4)
    kvs = jnp.concatenate([cached, fresh], axis=3).reshape(NCTX, 128, HD)
    x3 = mamba_x.transpose(1, 0, 2)
    xt = x3.reshape(T * R, C)
    rs = x3[T - 3 :].reshape(3, R, 2, C // 2).transpose(0, 2, 1, 3).reshape(3, 2 * R, C // 2)
    dtt = dt_raw.transpose(1, 0, 2).reshape(T * R, C)
    cs = conv_state.transpose(1, 0, 2).reshape(3 * R, C).astype(F32)
    cwb = jnp.concatenate(
        [conv_weight, conv_bias[None], skip_gain[None], jnp.zeros((2, C), F32)], axis=0
    )
    xp = jnp.pad(x_proj.T, ((0, 0), (0, 128 - 2 * S)))
    a2 = -jnp.exp(a_log) * LOG2E
    a2o = jnp.repeat(lax.dynamic_slice_in_dim(a2, c * 128, 128, 1), R, axis=0)
    s0 = lax.dynamic_slice_in_dim(ssm_state, c * 128, 128, 2)
    s0 = s0.transpose(1, 0, 2).reshape(S * R, 128).astype(F32)
    mine = c // 2
    clen, nlen = cached_len[0, mine], new_len[0, mine]
    block = jnp.arange(NCTX, dtype=jnp.int32)[:, None]
    never = jnp.int32(1 << 20)
    cpos = block * SPAN + jnp.arange(SPAN, dtype=jnp.int32)[None]
    npos = block * T + jnp.arange(T, dtype=jnp.int32)[None]
    thr = jnp.concatenate(
        [jnp.where(cpos < clen, -1, never), jnp.where(npos < nlen, npos, never)], axis=1
    ).reshape(1, NCTX * 64)
    nlr = jnp.broadcast_to(new_len[0][:, None], (R, 128))
    slots = jnp.arange(NREQ, dtype=jnp.int32)
    order = jnp.sum(
        jnp.where(target_group[0][None, :] == slots[:, None], slots[None, :], 0), axis=1
    )
    meta = jnp.concatenate([order, nlen[None]]).astype(jnp.int32)

    vmem = pl.BlockSpec(memory_space=pltpu.VMEM)
    smem = pl.BlockSpec(memory_space=pltpu.SMEM)
    dma = pltpu.SemaphoreType.DMA
    att, mix = pl.pallas_call(
        kernel,
        out_shape=(
            jax.ShapeDtypeStruct((NREQ, 2 * T * 8, HD), BF16),
            jax.ShapeDtypeStruct((NREQ, T, C), BF16),
        ),
        in_specs=[vmem] * 13 + [smem],
        out_specs=(vmem, vmem),
        scratch_shapes=[
            pltpu.VMEM((NCTX, 128, HD), BF16),
            pltpu.VMEM((NCTX, 128, HD), BF16),
            pltpu.VMEM((3, 2 * R, C // 2), BF16),
            pltpu.VMEM((3 * R, C), F32),
            pltpu.VMEM((T * R, C), F32),
            pltpu.VMEM((T * R, C), BF16),
            pltpu.VMEM((T * R, C), F32),
            pltpu.VMEM((T * R, 128), F32),
            pltpu.VMEM((NTP - 1, T * R, 128), F32),
            pltpu.VMEM((T * S, R, 128), F32),
            pltpu.VMEM((T * S, R, 128), F32),
            pltpu.VMEM((TILES * T * S, R, 128), F32),
            pltpu.VMEM((T * R, C), F32),
            pltpu.VMEM((TILES, T * R, 128), F32),
            pltpu.VMEM((NCTX, S * R + 2 * R, 128), BF16),
            pltpu.VMEM((NCTX, S * R + 2 * R, 128), BF16),
            pltpu.VMEM((NCTX, S * R, 128), BF16),
            pltpu.VMEM((NCTX, S * R, 128), BF16),
            pltpu.VMEM((NCTX, 128, HD), BF16),
            pltpu.VMEM((NCTX, 128, HD), BF16),
            pltpu.VMEM((NREQ, T, C), BF16),
            pltpu.VMEM((NREQ, 2 * T * 8, HD), BF16),
            pltpu.VMEM((R, T, C), BF16),
            pltpu.VMEM((R, 2 * T * 8, HD), BF16),
            dma((5, NCTX)),
            dma((5, NCTX)),
            dma,
            dma,
            dma((NTP,)),
            dma((NTP,)),
            dma((2, NREQ)),
            dma((2, NREQ)),
        ],
        compiler_params=pltpu.CompilerParams(
            collective_id=0, has_side_effects=True, vmem_limit_bytes=56 << 20
        ),
    )(qs, kvs, rs, xt, dtt, cwb, cs, xp, a2, a2o, s0, thr, nlr, meta)
    return att.reshape(NREQ, T, 16, HD), mix


def solution(mesh):
    in_specs = (
        P("req", "ctx", "tp", None),
        P(None, "req", "ctx", None, "tp", None),
        P(None, "req", "ctx", "tp", None),
        P("req", "ctx", None),
        P("req", None),
        P("req", None),
        P("req", "ctx", "tp"),
        P("req", None, "tp"),
        P(None, "tp"),
        P("tp"),
        P(None, "tp"),
        P("req", "ctx", "tp"),
        P(None, "tp"),
        P("tp"),
        P("req", None, "tp"),
        P("req", None),
    )
    out_specs = (P("req", "ctx", "tp", None), P("req", "ctx", "tp"))
    return jax.shard_map(
        per_device, mesh=mesh, in_specs=in_specs, out_specs=out_specs, check_vma=False
    )
```

time: 673 us -> 188 us (0.28)
  the two profiles are of different devices: /device:TPU:6 before, /device:TPU:97 now
where the time goes in v1:
time: 188 us
  Pallas kernels  167 us (89%)
  local copies, waits for them, and re-layouts  13.4 us (7%)
  other arithmetic  5.9 us (3%)
    pallas_call x1, Pallas kernels, per_device(): pl.pallas_call(kernel, out_shape=(jax.ShapeDtypeStruct((NREQ, 2 * T * 8,...  167 us
    unnamed x40, local copies, waits for them, and re-layouts  4.64 us

profile of v1, /device:TPU:97, one launch (start us, length us, event | category | flops | bytes accessed | tf_op | source)
XLA Modules:
  0.0 187.6 jit_solution(15371283466945527919)
XLA Ops:
  0.6 0.0 copy-start.16
  0.7 0.0 copy-start.15
  0.7 0.0 copy-start.13
  0.7 0.0 copy-start.14
  0.7 0.5 broadcast.64
  1.2 0.1 copy-done.16
  1.3 0.7 reduce.3
  2.0 0.0 copy-start.11
  2.0 0.0 copy-done.15
  2.0 0.0 copy-start.10
  2.0 0.1 select_reduce_fusion
  2.1 0.1 pad.12.clone
  2.2 0.0 copy-done.13
  2.2 0.0 copy-done.14
  2.2 0.6 constant_dynamic-slice_fusion
  2.8 1.2 pad_add_fusion.1.meta
  4.1 0.1 squeeze.14
  4.1 0.7 broadcast_in_dim.74.nlr
  4.8 0.1 broadcast_in_dim.62
  4.9 0.1 broadcast_in_dim.63
  5.0 0.7 compare_select_fusion
  5.7 0.7 fusion.1
  6.4 0.1 pad_add_fusion
  6.5 0.7 reshape.99.thr
  7.2 0.0 copy-done.12
  7.2 0.0 copy-done.11
  7.2 0.0 copy-done.10
  7.2 0.7 maximum_maximum_fusion.cwb
  7.9 0.8 convert_bitcast_fusion.1
  8.6 0.0 copy-done.7
  8.7 0.0 copy-start.1
  8.7 0.0 copy-start.8
  8.7 0.7 copy_bitcast_fusion.5
  9.4 0.3 copy-done.8
  9.7 0.0 copy-done.1
  9.7 0.0 copy-done
  9.7 0.0 copy-start.9
  9.7 0.1 slice.6
  9.8 0.0 copy-start.5
  9.8 0.1 reshape.111
  9.9 0.7 copy.66
  10.6 0.0 copy-done.9
  10.6 0.7 convert_bitcast_fusion.cs
  11.3 0.0 copy-done.5
  11.3 0.1 copy.64
  11.4 0.6 gather_fusion
  12.0 0.1 copy.47
  12.1 0.1 fusion
  12.2 0.1 pad_maximum_fusion
  12.3 0.0 copy-start.2
  12.3 0.8 copy.49
  13.1 0.4 copy-done.2
  13.5 0.9 copy.45
  14.4 0.0 copy-done.6
  14.4 0.3 copy.54
  14.7 0.0 copy-start.4
  14.7 0.9 pad.4.xp
  15.7 0.2 copy-done.4
  15.8 1.6 copy_bitcast_fusion
  17.4 167.4 %shard_map.167 = (bf16[8,256,128]{2,1,0:T(8,128)(2,1)}, bf16[8,16,2048]{2,1,0:T(8,128)(2,1)}) custom-call(bf16[16,128,128]{2,1,0:T(8,128)(2,1)} %bitcast.57, bf16[16,128,128]{2,1,0:T(8,128)(2,1)} %bitcast.56, bf16[3,16,1024]{2,1,0:T(8,128)(2,1)} %bitcast.67, bf16[128,2048]{1,0:T(8,128)(2,1)} %get-tuple-element.9.xt, bf16[128,2048]{1,0:T(8,128)(2,1)} %get-tuple-element.8.dtt, ...), custom_call_target="tpu_custom_call" | custom-call | tf_op jit(solution)/shard_map/pallas_call | solution.py:399
  184.8 0.0 copy-start.3
  184.9 1.9 %copy.69 = bf16[8,16,16,128]{3,2,1,0:T(8,128)(2,1)} copy(bf16[8,16,16,128]{3,2,1,0:T(8,128)(2,1)} %bitcast.64) | data formatting | bytes 1048576
  186.8 0.0 copy-done.3
  186.8 0.8 copy.70
  (13 shorter events, 0.1 us)
Async XLA Ops:
  0.6 0.7 copy-start.16
  0.7 1.3 copy-start.15
  0.7 1.6 copy-start.13
  0.7 1.6 copy-start.14
  1.3 5.9 %copy-start.12 = (f32[2048]{0:T(1024)S(1)}, f32[2048]{0:T(1024)}, u32[]{:S(2)}) copy-start(f32[2048]{0:T(1024)} %param.25) | copy-start | bytes 24580
  2.0 5.2 %copy-start.11 = (f32[2048]{0:T(1024)S(1)}, f32[2048]{0:T(1024)}, u32[]{:S(2)}) copy-start(f32[2048]{0:T(1024)} %param.29) | copy-start | bytes 24580
  2.0 5.2 %copy-start.10 = (f32[4,2048]{1,0:T(4,128)S(1)}, f32[4,2048]{1,0:T(4,128)}, u32[]{:S(2)}) copy-start(f32[4,2048]{1,0:T(4,128)} %param.24) | copy-start | bytes 98308
  4.1 4.6 %copy-start.7 = (f32[16,2048]{1,0:T(8,128)S(1)}, f32[16,2048]{1,0:T(8,128)}, u32[]{:S(2)}) copy-start(f32[16,2048]{1,0:T(8,128)} %param.28) | copy-start | bytes 393220
  4.1 5.6 %copy-start = (bf16[8,16,2048]{2,1,0:T(8,128)(2,1)S(1)}, bf16[8,16,2048]{2,1,0:T(8,128)(2,1)}, u32[]{:S(2)}) copy-start(bf16[8,16,2048]{2,1,0:T(8,128)(2,1)} %param.22) | copy-start | bytes 1572868
  8.7 1.0 copy-start.1
  8.7 1.0 copy-start.8
  9.7 0.9 copy-start.9
  9.8 1.5 copy-start.5
  12.3 1.2 copy-start.2
  13.5 0.9 copy-start.6
  14.7 1.1 copy-start.4
  184.8 1.9 %copy-start.3 = (bf16[8,16,2048]{2,1,0:T(8,128)(2,1)S(1)}, bf16[8,16,2048]{2,1,0:T(8,128)(2,1)}, u32[]{:S(2)}) copy-start(bf16[8,16,2048]{2,1,0:T(8,128)(2,1)} %get-tuple-element.15) | copy-start | bytes 1572868

commit v2 on v1

v2 whole, which is shorter than its diff:
```python
import math

import jax
import jax.numpy as jnp
from jax import lax
from jax.experimental import pallas as pl
from jax.experimental.pallas import tpu as pltpu
from jax.sharding import PartitionSpec as P

MESH = pl.DeviceIdType.MESH
F32 = jnp.float32
BF16 = jnp.bfloat16
LOG2E = math.log2(math.e)
NREQ, NCTX, NTP = 8, 16, 4
R, T, C, S = 8, 16, 2048, 16
HD = 128
PAGE, PAGES_REQ = 8, 6
SPAN = PAGE * PAGES_REQ
TILES = C // 128
QU, KV, ST, PF = range(4)


def wrap(a, n):
    return lax.rem(a + n, n)


def tile_lanes(j):
    return pl.ds(pl.multiple_of(j * 128, 128), 128)


def copy_to(axis, peer, src, dst, send_sem, recv_sem):
    return pltpu.make_async_remote_copy(
        src_ref=src,
        dst_ref=dst,
        send_sem=send_sem,
        recv_sem=recv_sem,
        device_id={axis: peer},
        device_id_type=MESH,
    )


def ctx_step(c, k, sign):
    dx, m = k // 4, lax.rem(k, 4)
    dz = lax.rem(2 * m, 4) + m // 2
    x, z = c // 4, lax.rem(c, 4)
    return wrap(x + sign * dx, 4) * 4 + wrap(z + sign * dz, 4)


def kernel(
    q_ref, pool, fresh, x_ref, dt_ref, taps_ref, bias, gains, a_log, old_x, xp, ssm,
    table, clens, nlens, target,
    att, mix,
    xf, df, q_s, q_r, kv_s, kv_r, rs, rr, rf, a2, xc, xcb, dts, pp, pr, pj,
    bb, cb, av, yl, yr, s0,
    st_s, st_r, pf_s, pf_r, ao_s, ao_r, y_s, y_all, order,
    ctx_send, ctx_recv, out_send, out_recv, rim_send, rim_recv,
    tp_send, tp_recv, req_send, req_recv,
):
    g, c, p = lax.axis_index("req"), lax.axis_index("ctx"), lax.axis_index("tp")
    slot, key_head = c // 2, lax.rem(c, 2)

    barrier = pltpu.get_barrier_semaphore()
    for axis, me, n in (("ctx", c, NCTX), ("tp", p, NTP), ("req", g, NREQ)):

        def greet(k, carry, axis=axis, me=me, n=n):
            pl.semaphore_signal(
                barrier, inc=1, device_id={axis: wrap(me + k, n)}, device_id_type=MESH
            )
            return carry

        lax.fori_loop(1, n, greet, 0)

    def greet_owner(k, carry):
        pl.semaphore_signal(
            barrier,
            inc=1,
            device_id={"req": k // 2, "ctx": 2 * g + lax.rem(k, 2)},
            device_id_type=MESH,
        )
        return carry

    lax.fori_loop(0, 2 * NREQ, greet_owner, 0)
    def convert(j, carry):
        lanes = tile_lanes(j)
        xf[j] = x_ref[:, :, lanes].astype(F32).reshape(R * T, 128)
        df[j] = dt_ref[:, :, lanes].astype(F32).reshape(R * T, 128)
        return carry

    lax.fori_loop(0, TILES, convert, 0)
    for k in range(3):
        tiles = [xf[j, pl.ds(T - 3 + k, R, stride=T), :] for j in range(TILES)]
        halves = [
            jnp.concatenate(tiles[: TILES // 2], axis=1),
            jnp.concatenate(tiles[TILES // 2 :], axis=1),
        ]
        rs[k] = jnp.concatenate(halves, axis=0).astype(BF16)

    for taker in range(NREQ):
        found = jnp.int32(0)
        for i in range(1, R):
            found = jnp.where(target[i] == taker, i, found)
        order[taker] = found

    def fill(o, carry):
        i = order[o]
        parts = [[[], []], [[], []]]
        for n in range(PAGES_REQ):
            page = table[i, n]
            for head in range(2):
                both = pool[page, head].astype(F32)
                for kind in range(2):
                    parts[head][kind].append(both[kind * PAGE : kind * PAGE + PAGE])
        new = fresh[i]
        for head in range(2):
            for kind in range(2):
                at = kind * 64
                rows = jnp.concatenate(parts[head][kind], axis=0).astype(BF16)
                kv_s[2 * o + head, at : at + SPAN] = rows
                kv_s[2 * o + head, at + SPAN : at + 64] = new[head, kind]
        return carry

    lax.fori_loop(0, R, fill, 0)

    pl.semaphore_wait(barrier, NCTX + NTP + NREQ - 3 + 2 * NREQ)

    def ctx_copy(kind, k, src, dst):
        return copy_to(
            "ctx", ctx_step(c, k, 1), src, dst, ctx_send.at[kind, k], ctx_recv.at[kind, k]
        )

    def ctx_wait_recv(kind, dst):
        def one(k, carry):
            place = dst.at[ctx_step(c, k, -1)]
            ctx_copy(kind, k, place, place).wait_recv()
            return carry

        lax.fori_loop(1, NCTX, one, 0)

    def ctx_wait_send(kind, src):
        def one(k, carry):
            place = src.at[ctx_step(c, k, 1)]
            ctx_copy(kind, k, place, place).wait_send()
            return carry

        lax.fori_loop(1, NCTX, one, 0)

    rim = copy_to("ctx", wrap(c + 1, NCTX), rs, rr, rim_send, rim_recv)
    rim.start()

    def send_kv(k, carry):
        ctx_copy(KV, k, kv_s.at[ctx_step(c, k, 1)], kv_r.at[c]).start()
        return carry

    lax.fori_loop(1, NCTX, send_kv, 0)
    kv_r[c] = kv_s[c]

    def fill_queries(o, carry):
        q = q_ref[order[o]].astype(F32)
        for head in range(2):
            rows = q[:, head * 8 : head * 8 + 8].reshape(T * 8, HD)
            q_s[2 * o + head] = rows.astype(BF16)
        return carry

    lax.fori_loop(0, R, fill_queries, 0)
    a2[...] = jnp.exp(a_log[...]) * (-LOG2E)

    def soften(j, carry):
        lanes = tile_lanes(j)
        for t in range(T):
            d = df[j, pl.ds(t, R, stride=T), :]
            soft = jnp.maximum(d, 0.0) + jnp.log1p(jnp.exp(-jnp.abs(d)))
            dts[t * R : t * R + R, lanes] = soft
        return carry

    lax.fori_loop(0, TILES, soften, 0)

    rim.wait_recv()
    for k in range(3):
        got = rr[k].astype(F32)
        rows = slice(k * R, k * R + R)
        for half in range(2):
            rf[rows, half * 1024 : half * 1024 + 1024] = got[half * R : half * R + R]

    @pl.when(c == 0)
    def _():
        for k in range(3):
            rf[k * R : k * R + R, :] = old_x[k].astype(F32)

    def convolve(j, carry):
        lanes = tile_lanes(j)
        rows = [rf[k * R : k * R + R, lanes] for k in range(3)]
        rows += [xf[j, pl.ds(t, R, stride=T), :] for t in range(T)]
        taps = [jnp.broadcast_to(taps_ref[k : k + 1, lanes], (R, 128)) for k in range(4)]
        shift = jnp.broadcast_to(bias[0:1, lanes], (R, 128))
        outs = []
        for t in range(T):
            total = taps[0] * rows[t]
            for k in range(1, 4):
                total = total + taps[k] * rows[t + k]
            total = total + shift
            outs.append(total / (1.0 + jnp.exp(-total)))
        rounded = jnp.concatenate(outs, axis=0).astype(BF16)
        xcb[:, lanes] = rounded
        xc[:, lanes] = rounded.astype(F32)
        return carry

    lax.fori_loop(0, TILES, convolve, 0)

    pp[...] = lax.dot_general(
        xp[...], xcb[...], (((1,), (1,)), ((), ())), preferred_element_type=F32
    )
    for k in range(1, NTP):
        copy_to("tp", wrap(p + k, NTP), pp, pr.at[k - 1], tp_send.at[k], tp_recv.at[k]).start()
    for k in range(1, NTP):
        copy_to("tp", wrap(p + k, NTP), pp, pr.at[k - 1], tp_send.at[k], tp_recv.at[k]).wait()
    pj[...] = jnp.transpose((pp[...] + pr[0]) + (pr[1] + pr[2]), (1, 0))

    def spread(t, carry):
        rows = pj[pl.ds(pl.multiple_of(t * R, R), R), :]
        for s in range(S):
            bb[t * S + s] = jnp.broadcast_to(rows[:, s : s + 1], (R, 128))
            cb[t * S + s] = jnp.broadcast_to(rows[:, S + s : S + s + 1], (R, 128))
        return carry

    lax.fori_loop(0, T, spread, 0)

    def scan_tile(k, carry):
        j = ctx_step(c, k, 1)
        lanes = tile_lanes(j)
        rate = [jnp.broadcast_to(a2[s : s + 1, lanes], (R, 128)) for s in range(S)]
        gain = jnp.broadcast_to(gains[0:1, lanes], (R, 128))

        def step(t, carry):
            elapsed, state = carry[0], carry[1:]
            rows = pl.ds(pl.multiple_of(t * R, R), R)
            d, x = dts[rows, lanes], xc[rows, lanes]
            u = d * x
            parts = [gain * x, None]
            new = []
            for s in range(S):
                decay = jnp.exp2(d * rate[s])
                av[j * (T * S) + t * S + s] = decay
                h = decay * state[s] + u * bb[t * S + s]
                new.append(h)
                y = cb[t * S + s] * h
                parts[s % 2] = y if parts[s % 2] is None else parts[s % 2] + y
            yl[rows, lanes] = parts[0] + parts[1]
            return (elapsed + d, *new)

        zero = jnp.zeros((R, 128), F32)
        last = lax.fori_loop(0, T, step, (zero,) * (S + 1))
        high = last[0].astype(BF16).astype(F32)
        packed = jnp.concatenate([*last[1:], high, last[0] - high], axis=0).astype(BF16)
        st_s[j] = packed

        @pl.when(k > 0)
        def _():
            ctx_copy(ST, k, st_s.at[j], st_r.at[c]).start()

        @pl.when(k == 0)
        def _():
            st_r[c] = packed

        return carry

    lax.fori_loop(0, NCTX, scan_tile, 0)

    def send_queries(k, carry):
        ctx_copy(QU, k, q_s.at[ctx_step(c, k, 1)], q_r.at[c]).start()
        return carry

    lax.fori_loop(1, NCTX, send_queries, 0)
    q_r[c] = q_s[c]

    ctx_wait_recv(ST, st_r)

    lanes_c = tile_lanes(c)
    s0[...] = ssm[:, :, lanes_c].astype(F32).reshape(R * S, 128)
    rates = jnp.concatenate(
        [jnp.broadcast_to(a2[s : s + 1, lanes_c], (R, 128)) for s in range(S)], axis=0
    )
    start = jnp.concatenate([s0[pl.ds(s, R, stride=S), :] for s in range(S)], axis=0)

    def advance(b, state):
        pf_s[b] = state.astype(BF16)
        item = st_r[b].astype(F32)
        elapsed = item[S * R : S * R + R] + item[S * R + R :]
        return jnp.exp2(rates * jnp.concatenate([elapsed] * S, axis=0)) * state + item[: S * R]

    lax.fori_loop(0, NCTX, advance, start)

    def send_prefix(k, carry):
        peer = ctx_step(c, k, 1)
        ctx_copy(PF, k, pf_s.at[peer], pf_r.at[c]).start()
        return carry

    lax.fori_loop(1, NCTX, send_prefix, 0)
    pf_r[c] = pf_s[c]

    ctx_wait_recv(KV, kv_r)
    ctx_wait_recv(QU, q_r)
    own = order[slot]
    own_cached, own_len = clens[own], nlens[own]
    factor = HD**-0.5 * LOG2E
    key = lax.broadcasted_iota(jnp.int32, (1, NCTX * 64), 1)
    block, spot = key // 64, lax.rem(key, 64)
    never = jnp.int32(1 << 20)
    cached_from = jnp.where(block * SPAN + spot < own_cached, -1, never)
    fresh_at = block * T + spot - SPAN
    fresh_from = jnp.where(fresh_at < own_len, fresh_at, never)
    seen_from = jnp.where(spot < SPAN, cached_from, fresh_from)

    def out_copy(peer, src):
        return pltpu.make_async_remote_copy(
            src_ref=src,
            dst_ref=ao_r.at[2 * g + key_head],
            send_sem=out_send.at[peer],
            recv_sem=out_recv.at[2 * g + key_head],
            device_id={"req": slot, "ctx": peer},
            device_id_type=MESH,
        )

    def is_me(peer):
        return jnp.logical_and(slot == g, peer == c)

    def attend(k, carry):
        b = wrap(slot + k, NCTX // 2)
        q = q_r[pl.ds(2 * b, 2)].reshape(2 * T * 8, HD)
        keys = kv_r[:, 0:64, :].reshape(NCTX * 64, HD)
        values = kv_r[:, 64:128, :].reshape(NCTX * 64, HD)
        scores = lax.dot_general(
            q, keys, (((1,), (1,)), ((), ())), preferred_element_type=F32
        )
        row = lax.broadcasted_iota(jnp.int32, (2 * T * 8, 1), 0)
        when = b * (2 * T) + row // 8
        scores = jnp.where(when >= seen_from, scores, -1e30)
        top = jnp.max(scores, axis=1, keepdims=True)
        weight = jnp.exp2((scores - top) * factor)
        total = jnp.sum(weight, axis=1, keepdims=True)
        out = jnp.dot(weight.astype(BF16), values, preferred_element_type=F32) / total
        out = jnp.where(when < own_len, out, 0.0).astype(BF16)
        for half in range(2):
            peer = 2 * b + half
            part = out[half * T * 8 : (half + 1) * T * 8]
            ao_s[peer] = part

            @pl.when(jnp.logical_not(is_me(peer)))
            def _():
                out_copy(peer, ao_s.at[peer]).start()

            @pl.when(is_me(peer))
            def _():
                ao_r[2 * g + key_head] = part

        return carry

    lax.fori_loop(0, NCTX // 2, attend, 0)

    request = lax.broadcasted_iota(jnp.int32, (R, 128), 0)
    limits = jnp.zeros((R, 128), jnp.int32)
    for i in range(R):
        limits = jnp.where(request == i, nlens[i], limits)

    def finish_tile(k, carry):
        j = ctx_step(c, k, -1)
        lanes = tile_lanes(j)

        @pl.when(k > 0)
        def _():
            ctx_copy(PF, k, pf_r.at[j], pf_r.at[j]).wait_recv()

        begin = pf_r[j].astype(F32)

        def step(t, state):
            rows = pl.ds(pl.multiple_of(t * R, R), R)
            parts = [yl[rows, lanes], None]
            new = []
            for s in range(S):
                h = av[j * (T * S) + t * S + s] * state[s]
                new.append(h)
                y = cb[t * S + s] * h
                parts[s % 2] = y if parts[s % 2] is None else parts[s % 2] + y
            y = jnp.where(c * T + t < limits, parts[0] + parts[1], 0.0)
            yr[j, pl.ds(t, R, stride=T), :] = y
            return tuple(new)

        lax.fori_loop(0, T, step, tuple(begin[s * R : s * R + R] for s in range(S)))
        return carry

    lax.fori_loop(0, NCTX, finish_tile, 0)

    def join_tiles(i, carry):
        rows = yr[:, pl.ds(pl.multiple_of(i * T, T), T), :]
        y_all[i] = jnp.concatenate([rows[j] for j in range(TILES)], axis=1).astype(BF16)
        return carry

    lax.fori_loop(0, R, join_tiles, 0)

    def req_copy(k, src, dst):
        return copy_to("req", wrap(g + k, NREQ), src, dst, req_send.at[k], req_recv.at[k])

    def give_mixed(k, carry):
        taker = wrap(g + k, NREQ)
        i = order[taker]
        rows = y_all[i]

        @pl.when(k > 0)
        def _():
            y_s[taker] = rows
            req_copy(k, y_s.at[taker], mix.at[g]).start()

        @pl.when(k == 0)
        def _():
            mix[g] = rows

        return carry

    lax.fori_loop(0, NREQ, give_mixed, 0)

    def land(source, carry):
        own_part = jnp.logical_and(
            source // 2 == g, 2 * g + lax.rem(source, 2) == c
        )

        @pl.when(jnp.logical_not(own_part))
        def _():
            place = ao_r.at[source]
            pltpu.make_async_remote_copy(
                src_ref=place,
                dst_ref=place,
                send_sem=out_send.at[source],
                recv_sem=out_recv.at[source],
                device_id={"req": slot, "ctx": source},
                device_id_type=MESH,
            ).wait_recv()

        return carry

    lax.fori_loop(0, 2 * NREQ, land, 0)

    def join_heads(i, carry):
        heads = [
            ao_r[2 * i + half].astype(F32).reshape(T, 8, HD) for half in range(2)
        ]
        att[i] = jnp.concatenate(heads, axis=1).astype(BF16)
        return carry

    lax.fori_loop(0, NREQ, join_heads, 0)

    rim.wait_send()
    for kind, src in ((QU, q_s), (KV, kv_s), (ST, st_s), (PF, pf_s)):
        ctx_wait_send(kind, src)

    def sent(peer, carry):
        @pl.when(jnp.logical_not(is_me(peer)))
        def _():
            out_copy(peer, ao_s.at[peer]).wait_send()

        return carry

    lax.fori_loop(0, NCTX, sent, 0)

    def last(k, carry):
        taker, giver = wrap(g + k, NREQ), wrap(g - k, NREQ)
        req_copy(k, y_s.at[taker], mix.at[giver]).wait()
        return carry

    lax.fori_loop(1, NREQ, last, 0)


def per_device(
    queries,
    kv_pool,
    new_kv,
    block_table,
    cached_len,
    new_len,
    mamba_x,
    conv_state,
    conv_weight,
    conv_bias,
    x_proj,
    dt_raw,
    a_log,
    skip_gain,
    ssm_state,
    target_group,
):
    pool = kv_pool[:, 0].transpose(1, 3, 0, 2, 4).reshape(-1, 2, 2 * PAGE, HD)
    fresh = new_kv.transpose(1, 3, 0, 2, 4)
    vmem = pl.BlockSpec(memory_space=pltpu.VMEM)
    smem = pl.BlockSpec(memory_space=pltpu.SMEM)
    dma = pltpu.SemaphoreType.DMA
    att, mix = pl.pallas_call(
        kernel,
        out_shape=(
            jax.ShapeDtypeStruct((NREQ, T, 16, HD), BF16),
            jax.ShapeDtypeStruct((NREQ, T, C), BF16),
        ),
        in_specs=[vmem] * 12 + [smem] * 4,
        out_specs=(vmem, vmem),
        scratch_shapes=[
            pltpu.VMEM((TILES, R * T, 128), F32),
            pltpu.VMEM((TILES, R * T, 128), F32),
            pltpu.VMEM((NCTX, 128, HD), BF16),
            pltpu.VMEM((NCTX, 128, HD), BF16),
            pltpu.VMEM((NCTX, 128, HD), BF16),
            pltpu.VMEM((NCTX, 128, HD), BF16),
            pltpu.VMEM((3, 2 * R, C // 2), BF16),
            pltpu.VMEM((3, 2 * R, C // 2), BF16),
            pltpu.VMEM((3 * R, C), F32),
            pltpu.VMEM((S, C), F32),
            pltpu.VMEM((T * R, C), F32),
            pltpu.VMEM((T * R, C), BF16),
            pltpu.VMEM((T * R, C), F32),
            pltpu.VMEM((2 * S, T * R), F32),
            pltpu.VMEM((NTP - 1, 2 * S, T * R), F32),
            pltpu.VMEM((T * R, 2 * S), F32),
            pltpu.VMEM((T * S, R, 128), F32),
            pltpu.VMEM((T * S, R, 128), F32),
            pltpu.VMEM((TILES * T * S, R, 128), F32),
            pltpu.VMEM((T * R, C), F32),
            pltpu.VMEM((TILES, T * R, 128), F32),
            pltpu.VMEM((R * S, 128), F32),
            pltpu.VMEM((NCTX, S * R + 2 * R, 128), BF16),
            pltpu.VMEM((NCTX, S * R + 2 * R, 128), BF16),
            pltpu.VMEM((NCTX, S * R, 128), BF16),
            pltpu.VMEM((NCTX, S * R, 128), BF16),
            pltpu.VMEM((NCTX, 128, HD), BF16),
            pltpu.VMEM((2 * NREQ, 128, HD), BF16),
            pltpu.VMEM((NREQ, T, C), BF16),
            pltpu.VMEM((R, T, C), BF16),
            pltpu.SMEM((NREQ,), jnp.int32),
            dma((4, NCTX)),
            dma((4, NCTX)),
            dma((NCTX,)),
            dma((2 * NREQ,)),
            dma,
            dma,
            dma((NTP,)),
            dma((NTP,)),
            dma((NREQ,)),
            dma((NREQ,)),
        ],
        compiler_params=pltpu.CompilerParams(
            collective_id=0, has_side_effects=True, vmem_limit_bytes=56 << 20
        ),
    )(
        queries, pool, fresh, mamba_x, dt_raw, conv_weight, conv_bias[None], skip_gain[None],
        a_log, conv_state.transpose(1, 0, 2), x_proj, ssm_state,
        block_table.reshape(R, PAGES_REQ), cached_len[0], new_len[0], target_group[0],
    )
    return att, mix


def solution(mesh):
    in_specs = (
        P("req", "ctx", "tp", None),
        P(None, "req", "ctx", None, "tp", None),
        P(None, "req", "ctx", "tp", None),
        P("req", "ctx", None),
        P("req", None),
        P("req", None),
        P("req", "ctx", "tp"),
        P("req", None, "tp"),
        P(None, "tp"),
        P("tp"),
        P(None, "tp"),
        P("req", "ctx", "tp"),
        P(None, "tp"),
        P("tp"),
        P("req", None, "tp"),
        P("req", None),
    )
    out_specs = (P("req", "ctx", "tp", None), P("req", "ctx", "tp"))
    return jax.shard_map(
        per_device, mesh=mesh, in_specs=in_specs, out_specs=out_specs, check_vma=False
    )
```

time: 188 us -> 175 us (0.931)
  the two profiles are of different devices: /device:TPU:97 before, /device:TPU:45 now
where the time goes in v2:
time: 175 us
  Pallas kernels  166 us (95%)
  local copies, waits for them, and re-layouts  7.42 us (4%)
    pallas_call x1, Pallas kernels, per_device(): pl.pallas_call(kernel, out_shape=(jax.ShapeDtypeStruct((NREQ, T, 16, HD),...  166 us
    unnamed x8, local copies, waits for them, and re-layouts  4.95 us

profile of v2, /device:TPU:45, one launch (start us, length us, event | category | flops | bytes accessed | tf_op | source)
XLA Modules:
  0.0 174.9 jit_solution(13806027145044684837)
XLA Ops:
  0.6 0.0 copy-start.1
  0.6 0.5 broadcast.3
  1.2 0.1 copy-done.1
  1.3 0.7 reduce.3
  2.0 0.7 reshape.11.table
  2.6 1.6 copy.23
  4.2 1.8 %copy.22 = bf16[48,2,2,8,128]{4,3,2,1,0:T(8,128)(2,1)} copy(bf16[48,2,2,8,128]{4,1,3,0,2:T(2,128)(2,1)} %bitcast.17) | data formatting | bytes 786432 | tf_op jit(solution)/shard_map/transpose | solution.py:489
  6.0 166.2 %shard_map.167 = (bf16[8,16,16,128]{3,2,1,0:T(8,128)(2,1)}, bf16[8,16,2048]{2,1,0:T(8,128)(2,1)}) custom-call(bf16[8,16,16,128]{3,2,1,0:T(8,128)(2,1)} %q_ref.1, bf16[48,2,16,128]{3,2,1,0:T(8,128)(2,1)} %bitcast.15, bf16[8,2,2,16,128]{4,3,2,1,0:T(8,128)(2,1)} %bitcast.16, bf16[8,16,2048]{2,1,0:T(8,128)(2,1)} %x_ref.1, bf16[8,16,2048]{2,1,0:T(8,128)(2,1)} %dt_ref.1, ...), custom_call_target="tpu_custom_call" | custom-call | tf_op jit(solution)/shard_map/pallas_call | solution.py:494
  172.2 0.0 copy-start
  172.2 1.9 %copy.26 = bf16[8,16,16,128]{3,2,1,0:T(8,128)(2,1)} copy(bf16[8,16,16,128]{3,2,1,0:T(8,128)(2,1)} %get-tuple-element.4) | data formatting | bytes 1048576
  174.1 0.0 copy-done
  174.1 0.8 copy.27
Async XLA Ops:
  0.6 0.7 copy-start.1
  172.2 1.9 %copy-start = (bf16[8,16,2048]{2,1,0:T(8,128)(2,1)S(1)}, bf16[8,16,2048]{2,1,0:T(8,128)(2,1)}, u32[]{:S(2)}) copy-start(bf16[8,16,2048]{2,1,0:T(8,128)(2,1)} %get-tuple-element.5) | copy-start | bytes 1572868

commit v3 on v2

--- a/solution.py
+++ b/solution.py
@@ -18,6 +18,7 @@
 SPAN = PAGE * PAGES_REQ
 TILES = C // 128
 QU, KV, ST, PF = range(4)
+EARLY_KV, EARLY_Q = 6, 5
 
 
 def wrap(a, n):
@@ -44,6 +45,12 @@
     dz = lax.rem(2 * m, 4) + m // 2
     x, z = c // 4, lax.rem(c, 4)
     return wrap(x + sign * dx, 4) * 4 + wrap(z + sign * dz, 4)
+
+
+def ctx_back(c, source):
+    dx = wrap(c // 4 - source // 4, 4)
+    dz = wrap(lax.rem(c, 4) - lax.rem(source, 4), 4)
+    return dx * 4 + lax.rem(2 * dz, 4) + dz // 2
 
 
 def kernel(
@@ -105,7 +112,7 @@
         i = order[o]
         parts = [[[], []], [[], []]]
         for n in range(PAGES_REQ):
-            page = table[i, n]
+            page = table[0, 0, i * PAGES_REQ + n]
             for head in range(2):
                 both = pool[page, head].astype(F32)
                 for kind in range(2):
@@ -151,7 +158,7 @@
         ctx_copy(KV, k, kv_s.at[ctx_step(c, k, 1)], kv_r.at[c]).start()
         return carry
 
-    lax.fori_loop(1, NCTX, send_kv, 0)
+    lax.fori_loop(1, EARLY_KV, send_kv, 0)
     kv_r[c] = kv_s[c]
 
     def fill_queries(o, carry):
@@ -211,6 +218,7 @@
     )
     for k in range(1, NTP):
         copy_to("tp", wrap(p + k, NTP), pp, pr.at[k - 1], tp_send.at[k], tp_recv.at[k]).start()
+    lax.fori_loop(EARLY_KV, NCTX, send_kv, 0)
     for k in range(1, NTP):
         copy_to("tp", wrap(p + k, NTP), pp, pr.at[k - 1], tp_send.at[k], tp_recv.at[k]).wait()
     pj[...] = jnp.transpose((pp[...] + pr[0]) + (pr[1] + pr[2]), (1, 0))
@@ -269,7 +277,7 @@
         ctx_copy(QU, k, q_s.at[ctx_step(c, k, 1)], q_r.at[c]).start()
         return carry
 
-    lax.fori_loop(1, NCTX, send_queries, 0)
+    lax.fori_loop(1, EARLY_Q, send_queries, 0)
     q_r[c] = q_s[c]
 
     ctx_wait_recv(ST, st_r)
@@ -296,9 +304,70 @@
 
     lax.fori_loop(1, NCTX, send_prefix, 0)
     pf_r[c] = pf_s[c]
+    lax.fori_loop(EARLY_Q, NCTX, send_queries, 0)
+
+    request = lax.broadcasted_iota(jnp.int32, (R, 128), 0)
+    limits = jnp.zeros((R, 128), jnp.int32)
+    for i in range(R):
+        limits = jnp.where(request == i, nlens[i], limits)
+
+    def finish_tile(k, carry):
+        j = ctx_step(c, k, -1)
+        lanes = tile_lanes(j)
+
+        @pl.when(k > 0)
+        def _():
+            ctx_copy(PF, k, pf_r.at[j], pf_r.at[j]).wait_recv()
+
+        begin = pf_r[j].astype(F32)
+
+        def step(t, state):
+            rows = pl.ds(pl.multiple_of(t * R, R), R)
+            parts = [yl[rows, lanes], None]
+            new = []
+            for s in range(S):
+                h = av[j * (T * S) + t * S + s] * state[s]
+                new.append(h)
+                y = cb[t * S + s] * h
+                parts[s % 2] = y if parts[s % 2] is None else parts[s % 2] + y
+            y = jnp.where(c * T + t < limits, parts[0] + parts[1], 0.0)
+            yr[j, pl.ds(t, R, stride=T), :] = y
+            return tuple(new)
+
+        lax.fori_loop(0, T, step, tuple(begin[s * R : s * R + R] for s in range(S)))
+        return carry
+
+    lax.fori_loop(0, NCTX, finish_tile, 0)
+
+    def join_tiles(i, carry):
+        rows = yr[:, pl.ds(pl.multiple_of(i * T, T), T), :]
+        y_all[i] = jnp.concatenate([rows[j] for j in range(TILES)], axis=1).astype(BF16)
+        return carry
+
+    lax.fori_loop(0, R, join_tiles, 0)
+
+    def req_copy(k, src, dst):
+        return copy_to("req", wrap(g + k, NREQ), src, dst, req_send.at[k], req_recv.at[k])
+
+    def give_mixed(k, carry):
+        taker = wrap(g + k, NREQ)
+        i = order[taker]
+        rows = y_all[i]
+
+        @pl.when(k > 0)
+        def _():
+            y_s[taker] = rows
+            req_copy(k, y_s.at[taker], mix.at[g]).start()
+
+        @pl.when(k == 0)
+        def _():
+            mix[g] = rows
+
+        return carry
+
+    lax.fori_loop(0, NREQ, give_mixed, 0)
 
     ctx_wait_recv(KV, kv_r)
-    ctx_wait_recv(QU, q_r)
     own = order[slot]
     own_cached, own_len = clens[own], nlens[own]
     factor = HD**-0.5 * LOG2E
@@ -324,7 +393,15 @@
         return jnp.logical_and(slot == g, peer == c)
 
     def attend(k, carry):
-        b = wrap(slot + k, NCTX // 2)
+        b = wrap(c // 4 - k // 2, 4) * 2 + lax.rem(k, 2)
+        for half in range(2):
+            source = 2 * b + half
+            step = ctx_back(c, source)
+
+            @pl.when(step > 0)
+            def _():
+                ctx_copy(QU, step, q_r.at[source], q_r.at[source]).wait_recv()
+
         q = q_r[pl.ds(2 * b, 2)].reshape(2 * T * 8, HD)
         keys = kv_r[:, 0:64, :].reshape(NCTX * 64, HD)
         values = kv_r[:, 64:128, :].reshape(NCTX * 64, HD)
@@ -355,67 +432,6 @@
         return carry
 
     lax.fori_loop(0, NCTX // 2, attend, 0)
-
-    request = lax.broadcasted_iota(jnp.int32, (R, 128), 0)
-    limits = jnp.zeros((R, 128), jnp.int32)
-    for i in range(R):
-        limits = jnp.where(request == i, nlens[i], limits)
-
-    def finish_tile(k, carry):
-        j = ctx_step(c, k, -1)
-        lanes = tile_lanes(j)
-
-        @pl.when(k > 0)
-        def _():
-            ctx_copy(PF, k, pf_r.at[j], pf_r.at[j]).wait_recv()
-
-        begin = pf_r[j].astype(F32)
-
-        def step(t, state):
-            rows = pl.ds(pl.multiple_of(t * R, R), R)
-            parts = [yl[rows, lanes], None]
-            new = []
-            for s in range(S):
-                h = av[j * (T * S) + t * S + s] * state[s]
-                new.append(h)
-                y = cb[t * S + s] * h
-                parts[s % 2] = y if parts[s % 2] is None else parts[s % 2] + y
-            y = jnp.where(c * T + t < limits, parts[0] + parts[1], 0.0)
-            yr[j, pl.ds(t, R, stride=T), :] = y
-            return tuple(new)
-
-        lax.fori_loop(0, T, step, tuple(begin[s * R : s * R + R] for s in range(S)))
-        return carry
-
-    lax.fori_loop(0, NCTX, finish_tile, 0)
-
-    def join_tiles(i, carry):
-        rows = yr[:, pl.ds(pl.multiple_of(i * T, T), T), :]
-        y_all[i] = jnp.concatenate([rows[j] for j in range(TILES)], axis=1).astype(BF16)
-        return carry
-
-    lax.fori_loop(0, R, join_tiles, 0)
-
-    def req_copy(k, src, dst):
-        return copy_to("req", wrap(g + k, NREQ), src, dst, req_send.at[k], req_recv.at[k])
-
-    def give_mixed(k, carry):
-        taker = wrap(g + k, NREQ)
-        i = order[taker]
-        rows = y_all[i]
-
-        @pl.when(k > 0)
-        def _():
-            y_s[taker] = rows
-            req_copy(k, y_s.at[taker], mix.at[g]).start()
-
-        @pl.when(k == 0)
-        def _():
-            mix[g] = rows
-
-        return carry
-
-    lax.fori_loop(0, NREQ, give_mixed, 0)
 
     def land(source, carry):
         own_part = jnp.logical_and(
@@ -548,7 +564,7 @@
     )(
         queries, pool, fresh, mamba_x, dt_raw, conv_weight, conv_bias[None], skip_gain[None],
         a_log, conv_state.transpose(1, 0, 2), x_proj, ssm_state,
-        block_table.reshape(R, PAGES_REQ), cached_len[0], new_len[0], target_group[0],
+        block_table, cached_len[0], new_len[0], target_group[0],
     )
     return att, mix
 

time: 175 us -> 176 us (level)
  the two profiles are of different devices: /device:TPU:45 before, /device:TPU:44 now
where the time goes in v3:
time: 176 us
  Pallas kernels  169 us (96%)
  local copies, waits for them, and re-layouts  6.1 us (3%)
    pallas_call x1, Pallas kernels, per_device(): pl.pallas_call(kernel, out_shape=(jax.ShapeDtypeStruct((NREQ, T, 16, HD),...  169 us
    unnamed x5, local copies, waits for them, and re-layouts  4.3 us

profile of v3, /device:TPU:44, one launch (start us, length us, event | category | flops | bytes accessed | tf_op | source)
XLA Modules:
  0.0 176.2 jit_solution(8527955286190364020)
XLA Ops:
  0.6 1.6 copy.23
  2.2 1.8 %copy.22 = bf16[48,2,2,8,128]{4,3,2,1,0:T(8,128)(2,1)} copy(bf16[48,2,2,8,128]{4,1,3,0,2:T(2,128)(2,1)} %bitcast.17) | data formatting | bytes 786432 | tf_op jit(solution)/shard_map/transpose | solution.py:505
  4.0 169.5 %shard_map.167 = (bf16[8,16,16,128]{3,2,1,0:T(8,128)(2,1)}, bf16[8,16,2048]{2,1,0:T(8,128)(2,1)}) custom-call(bf16[8,16,16,128]{3,2,1,0:T(8,128)(2,1)} %q_ref.1, bf16[48,2,16,128]{3,2,1,0:T(8,128)(2,1)} %bitcast.15, bf16[8,2,2,16,128]{4,3,2,1,0:T(8,128)(2,1)} %bitcast.16, bf16[8,16,2048]{2,1,0:T(8,128)(2,1)} %x_ref.1, bf16[8,16,2048]{2,1,0:T(8,128)(2,1)} %dt_ref.1, ...), custom_call_target="tpu_custom_call" | custom-call | tf_op jit(solution)/shard_map/pallas_call | solution.py:510
  173.5 0.0 copy-start
  173.5 1.9 %copy.26 = bf16[8,16,16,128]{3,2,1,0:T(8,128)(2,1)} copy(bf16[8,16,16,128]{3,2,1,0:T(8,128)(2,1)} %get-tuple-element.4) | data formatting | bytes 1048576
  175.4 0.0 copy-done
  175.4 0.8 copy.27
Async XLA Ops:
  173.5 1.9 %copy-start = (bf16[8,16,2048]{2,1,0:T(8,128)(2,1)S(1)}, bf16[8,16,2048]{2,1,0:T(8,128)(2,1)}, u32[]{:S(2)}) copy-start(bf16[8,16,2048]{2,1,0:T(8,128)(2,1)} %get-tuple-element.5) | copy-start | bytes 1572868

commit v4 on v0

v4 whole, which is shorter than its diff:
```python
import math

import jax
import jax.numpy as jnp
from jax import lax
from jax.experimental import pallas as pl
from jax.experimental.pallas import tpu as pltpu
from jax.sharding import PartitionSpec as P

MESH = pl.DeviceIdType.MESH
F32 = jnp.float32
BF16 = jnp.bfloat16
LOG2E = math.log2(math.e)
NREQ, NCTX, NTP = 8, 16, 4
R, T, C, S = 8, 16, 2048, 16
HD = 128
PAGE, PAGES_REQ = 8, 6
SPAN = PAGE * PAGES_REQ
TILES = C // 128
RUNS, RUN = 4, 2 * T
PAD = RUN + 3
X, D, KV, QU = range(4)


def wrap(a, n):
    return lax.rem(a + n, n)


class Owners:
    def __init__(self, c, shift):
        self.shift = shift
        self.x = c // 4
        self.ring = wrap(lax.rem(c, 4) - shift, 4)
        self.b = self.ring // 2
        self.slot = self.x * 2 + self.ring + self.b * (3 - 2 * self.ring)
        self.rank = self.x * 2 + lax.rem(self.ring, 2)
        self.partner = self.x * 4 + lax.rem(3 - self.ring + shift, 4)

    def owner(self, slot, b=None):
        b = self.b if b is None else b
        a = lax.rem(slot, 2)
        return (slot // 2) * 4 + lax.rem(a + b * (3 - 2 * a) + self.shift, 4)

    def block(self, rank, b=None):
        b = self.b if b is None else b
        return (rank // 2) * 4 + lax.rem(2 * b + lax.rem(rank, 2) + self.shift, 4)


def remote(device, src, dst, send_sem, recv_sem):
    return pltpu.make_async_remote_copy(
        src_ref=src,
        dst_ref=dst,
        send_sem=send_sem,
        recv_sem=recv_sem,
        device_id=device,
        device_id_type=MESH,
    )


def kernel(
    q_ref, pool, fresh, x_ref, dt_ref, taps_ref, bias, gains, a_log, old_x, xp, ssm,
    table, clens, nlens, target,
    att, mix,
    x_s, x_r, d_s, d_r, q_s, q_r, kv_s, kv_r, edge, edge_s, edge_r,
    taps, a2, xf, xc, dts, pp, pr, pj, sp, av, yl, s0, st_s, st_r, y_s, o_s, order,
    in_send, in_recv, edge_send, edge_recv, pass_send, pass_recv, st_send, st_recv,
    tp_send, tp_recv, out_send, out_recv,
):
    g, c, p = lax.axis_index("req"), lax.axis_index("ctx"), lax.axis_index("tp")
    z = lax.rem(c, 4)
    mine, heads = Owners(c, 0), Owners(c, 1)

    barrier = pltpu.get_barrier_semaphore()

    def greet(device):
        pl.semaphore_signal(barrier, inc=1, device_id=device, device_id_type=MESH)

    for who in (mine, heads):

        def greet_set(k, carry, who=who):
            greet({"ctx": who.owner(lax.rem(who.slot + k, R))})
            return carry

        def greet_givers(k, carry, who=who):
            greet({"req": k, "ctx": who.owner(wrap(g - k, NREQ))})
            return carry

        lax.fori_loop(1, R, greet_set, 0)
        greet({"ctx": who.partner})
        lax.fori_loop(0, NREQ, greet_givers, 0)
    for k in range(1, NTP):
        greet({"tp": wrap(p + k, NTP)})
    for k in range(RUNS):
        greet({"ctx": k * 4 + 3 - 2 * mine.b})

    for slot in range(NREQ):
        taker = lax.rem(g + slot, NREQ)
        found = jnp.int32(0)
        for i in range(1, R):
            found = jnp.where(target[i] == taker, i, found)
        order[slot] = found

    def fill_scan(o, carry):
        i = order[o]
        rows = x_ref[i]
        x_s[o] = rows
        d_s[o] = dt_ref[i]
        ends = rows.astype(F32)
        for j in range(TILES):
            for k in range(3):
                edge[k * TILES + j : k * TILES + j + 1, :] = ends[
                    T - 3 + k : T - 2 + k, j * 128 : j * 128 + 128
                ]
        edge_s[o] = edge[...].astype(BF16)
        return carry

    lax.fori_loop(0, R, fill_scan, 0)

    def fill_attention(o, carry):
        i = order[o]
        q_s[o] = q_ref[i].reshape(2 * T * 8, HD)
        parts = [[[], []], [[], []]]
        for n in range(PAGES_REQ):
            page = table[0, 0, i * PAGES_REQ + n]
            for head in range(2):
                both = pool[page, head].astype(F32)
                for kind in range(2):
                    parts[head][kind].append(both[kind * PAGE : kind * PAGE + PAGE])
        new = fresh[i]
        for head in range(2):
            for kind in range(2):
                at = head * 128 + kind * 64
                rows = jnp.concatenate(parts[head][kind], axis=0).astype(BF16)
                kv_s[o, at : at + SPAN] = rows
                kv_s[o, at + SPAN : at + 64] = new[head, kind]
        return carry

    lax.fori_loop(0, R, fill_attention, 0)

    pl.semaphore_wait(barrier, 2 * (R - 1 + 1 + NREQ) + NTP - 1 + R * lax.rem(z, 2))

    def in_copy(kind, who, slot, src, dst):
        return remote(
            {"ctx": who.owner(slot)},
            src.at[slot],
            dst.at[who.rank],
            in_send.at[kind, slot],
            in_recv.at[kind, who.rank],
        )

    def in_wait(kind, who, rank, dst):
        @pl.when(rank != who.rank)
        def _():
            place = dst.at[rank]
            remote(
                {"ctx": who.partner}, place, place, in_send.at[kind, rank], in_recv.at[kind, rank]
            ).wait_recv()

    inputs = ((X, mine, x_s, x_r), (KV, heads, kv_s, kv_r), (D, mine, d_s, d_r), (QU, heads, q_s, q_r))

    def edge_copy(slot):
        return remote(
            {"ctx": mine.owner(slot, 1 - mine.b)},
            edge_s.at[slot],
            edge_r.at[mine.x],
            edge_send.at[slot],
            edge_recv.at[mine.x],
        )

    @pl.when(lax.rem(z, 2) == 1)
    def _():
        def send_edge(o, carry):
            edge_copy(o).start()
            return carry

        lax.fori_loop(0, R, send_edge, 0)

    for pair in (inputs[:2], inputs[2:]):

        def send_pair(k, carry, pair=pair):
            for kind, who, src, dst in pair:
                in_copy(kind, who, lax.rem(who.slot + k, R), src, dst).start()
            return carry

        lax.fori_loop(1, R, send_pair, 0)
    for kind, who, src, dst in inputs:
        dst[who.rank] = src[who.slot]

    for j in range(TILES):
        lanes = slice(j * 128, j * 128 + 128)
        for k in range(4):
            taps[k * TILES + j : k * TILES + j + 1, :] = taps_ref[k : k + 1, lanes]
        taps[4 * TILES + j : 4 * TILES + j + 1, :] = bias[0:1, lanes]
        taps[5 * TILES + j : 5 * TILES + j + 1, :] = gains[0:1, lanes]
        a2[pl.ds(j, S, stride=TILES), :] = jnp.exp(a_log[:, lanes]) * (-LOG2E)
    own = order[mine.slot]
    old_state = ssm[own].astype(F32)
    for j in range(TILES):
        s0[pl.ds(j, S, stride=TILES), :] = old_state[:, j * 128 : j * 128 + 128]

    request = lax.broadcasted_iota(jnp.int32, (R, C), 0)
    for k in range(3):
        row = jnp.sum(jnp.where(request == own, old_x[k].astype(F32), 0.0), axis=0, keepdims=True)
        for j in range(TILES):
            edge[k * TILES + j : k * TILES + j + 1, :] = row[:, j * 128 : j * 128 + 128]

    def land_edge(i, carry):
        place = edge_r.at[i]
        remote({"ctx": mine.partner}, place, place, edge_send.at[i], edge_recv.at[i]).wait_recv()
        return carry

    lax.fori_loop(0, RUNS, land_edge, 0)
    leads = mine.b == 0
    before = edge[...]
    for i in range(RUNS):
        got = edge_r[i].astype(F32)
        xf[i * PAD * TILES : (i * PAD + 3) * TILES, :] = jnp.where(leads, before, got)
        before = got

    def land_x(n, carry):
        in_wait(X, mine, n, x_r)
        rows = x_r[n].astype(F32)
        at = ((n // 2) * PAD + 3 + lax.rem(n, 2) * T) * TILES
        for j in range(TILES):
            xf[pl.ds(at + j, T, stride=TILES), :] = rows[:, j * 128 : j * 128 + 128]
        return carry

    lax.fori_loop(0, R, land_x, 0)

    def convolve(m, carry):
        at = (m * 8 + (m // 4) * 3) * TILES
        total = jnp.zeros((8, TILES, 128), F32)
        for k in range(4):
            rows = xf[pl.ds(pl.multiple_of(at + k * TILES, TILES), 8 * TILES), :]
            weight = taps[k * TILES : k * TILES + TILES, :]
            total = total + weight[None] * rows.reshape(8, TILES, 128)
        total = total + taps[4 * TILES : 5 * TILES, :][None]
        out = (total / (1.0 + jnp.exp(-total))).astype(BF16).astype(F32)
        xc[pl.ds(pl.multiple_of(m * 8 * TILES, TILES), 8 * TILES), :] = out.reshape(8 * TILES, 128)
        return carry

    lax.fori_loop(0, R * T // 8, convolve, 0)

    total = jnp.zeros((2 * S, R * T), F32)
    for j in range(TILES):
        rows = xc[pl.ds(j, R * T, stride=TILES), :].astype(BF16)
        total = total + lax.dot_general(
            xp[:, j * 128 : j * 128 + 128],
            rows,
            (((1,), (1,)), ((), ())),
            preferred_element_type=F32,
        )
    pp[...] = total

    def tp_copy(k):
        return remote(
            {"tp": wrap(p + k, NTP)}, pp, pr.at[k - 1], tp_send.at[k], tp_recv.at[k]
        )

    for k in range(1, NTP):
        tp_copy(k).start()

    def pass_copy(n):
        return remote(
            {"ctx": heads.partner},
            kv_r.at[n],
            kv_r.at[R + n],
            pass_send.at[n],
            pass_recv.at[n],
        )

    def pass_on(n, carry):
        in_wait(KV, heads, n, kv_r)
        pass_copy(n).start()
        return carry

    lax.fori_loop(0, R, pass_on, 0)

    def land_d(n, carry):
        in_wait(D, mine, n, d_r)
        rows = d_r[n].astype(F32)
        soft = jnp.maximum(rows, 0.0) + jnp.log1p(jnp.exp(-jnp.abs(rows)))
        for j in range(TILES):
            dts[pl.ds(n * T * TILES + j, T, stride=TILES), :] = soft[:, j * 128 : j * 128 + 128]
        return carry

    lax.fori_loop(0, R, land_d, 0)

    for k in range(1, NTP):
        tp_copy(k).wait()
    pj[...] = jnp.transpose((pp[...] + pr[0]) + (pr[1] + pr[2]), (1, 0))
    for s in range(2 * S):
        sp[s * R * T : (s + 1) * R * T, :] = jnp.broadcast_to(pj[:, s : s + 1], (R * T, 128))

    def position(at):
        return pl.ds(pl.multiple_of(at * TILES, TILES), TILES)

    def spread(s, at):
        return jnp.broadcast_to(sp[pl.ds(s * (R * T) + at, 1), :], (TILES, 128))

    def st_copy(i):
        return remote(
            {"ctx": mine.partner}, st_s.at[i], st_r.at[i], st_send.at[i], st_recv.at[i]
        )

    def scan_run(i, carry):
        def step(t, carry):
            elapsed, state = carry[0], carry[1:]
            at = i * RUN + t
            d, x = dts[position(at), :], xc[position(at), :]
            u = d * x
            parts = [taps[5 * TILES : 6 * TILES, :] * x, None]
            new = []
            for s in range(S):
                decay = jnp.exp2(d * a2[s * TILES : s * TILES + TILES, :])
                av[at * S + s] = decay
                h = decay * state[s] + u * spread(s, at)
                new.append(h)
                y = spread(S + s, at) * h
                parts[s % 2] = y if parts[s % 2] is None else parts[s % 2] + y
            yl[position(at), :] = parts[0] + parts[1]
            return (elapsed + d, *new)

        zero = jnp.zeros((TILES, 128), F32)
        last = lax.fori_loop(0, RUN, step, (zero,) * (S + 1))
        high = last[0].astype(BF16).astype(F32)
        st_s[i] = jnp.concatenate([*last[1:], high, last[0] - high], axis=0).astype(BF16)
        st_copy(i).start()
        return carry

    lax.fori_loop(0, RUNS, scan_run, 0)

    def out_copy(kind, who, rank, src, dst):
        return remote(
            {"req": lax.rem(g + who.slot, NREQ), "ctx": who.block(rank)},
            src.at[rank],
            dst.at[g],
            out_send.at[kind, rank],
            out_recv.at[kind, g],
        )

    def stays(who, rank):
        return jnp.logical_and(who.slot == 0, rank == who.rank)

    def give(kind, who, rank, src, dst):
        @pl.when(jnp.logical_not(stays(who, rank)))
        def _():
            out_copy(kind, who, rank, src, dst).start()

        @pl.when(stays(who, rank))
        def _():
            dst[g] = src[rank]

    own_len = nlens[own]

    def finish_run(i, carry):
        st_copy(i).wait_recv()
        own_item, other = st_s[i].astype(F32), st_r[i].astype(F32)

        def advance(item, state):
            elapsed = item[S * TILES : (S + 1) * TILES] + item[(S + 1) * TILES :]
            decay = jnp.exp2(a2[...] * jnp.concatenate([elapsed] * S, axis=0))
            return decay * state + item[: S * TILES]

        ahead = s0[...]
        middle = advance(jnp.where(leads, own_item, other), ahead)
        s0[...] = advance(jnp.where(leads, other, own_item), middle)
        begin = jnp.where(leads, ahead, middle)

        def half(h, state):
            rank = i * 2 + h
            first = mine.block(rank) * T

            def step(t, state):
                at = rank * T + t
                parts = [yl[position(at), :], None]
                new = []
                for s in range(S):
                    h = av[at * S + s] * state[s]
                    new.append(h)
                    y = spread(S + s, at) * h
                    parts[s % 2] = y if parts[s % 2] is None else parts[s % 2] + y
                live = jnp.full((TILES, 128), first + t, jnp.int32) < own_len
                yl[position(at), :] = jnp.where(live, parts[0] + parts[1], 0.0)
                return tuple(new)

            state = lax.fori_loop(0, T, step, state)
            rows = [
                yl[pl.ds(rank * T * TILES + j, T, stride=TILES), :] for j in range(TILES)
            ]
            y_s[rank] = jnp.concatenate(rows, axis=1).astype(BF16)
            give(0, mine, rank, y_s, mix)
            return state

        lax.fori_loop(
            0, 2, half, tuple(begin[s * TILES : (s + 1) * TILES] for s in range(S))
        )
        return carry

    lax.fori_loop(0, RUNS, finish_run, 0)

    def land_kv(n, carry):
        pass_copy(n).wait_recv()
        return carry

    lax.fori_loop(0, R, land_kv, 0)
    asked = order[heads.slot]
    cached_len, new_len = clens[asked], nlens[asked]
    factor = HD**-0.5 * LOG2E
    key = lax.broadcasted_iota(jnp.int32, (1, NCTX * 64), 1)
    place, spot = key // 64, lax.rem(key, 64)
    rank = lax.rem(place, R)
    side = jnp.where(place < R, heads.b, 1 - heads.b)
    block = heads.block(rank, side)
    never = jnp.int32(1 << 20)
    cached_from = jnp.where(block * SPAN + spot < cached_len, -1, never)
    fresh_at = block * T + spot - SPAN
    fresh_from = jnp.where(fresh_at < new_len, fresh_at, never)
    seen_from = jnp.where(spot < SPAN, cached_from, fresh_from)

    def attend(k, carry):
        pair = wrap(heads.x - k, 4)
        for half in range(2):
            in_wait(QU, heads, 2 * pair + half, q_r)
        q = q_r[pl.ds(2 * pair, 2)].astype(F32).reshape(2 * T, 16, HD)
        row = lax.broadcasted_iota(jnp.int32, (2 * T * 8, 1), 0) // 8
        first, second = heads.block(2 * pair), heads.block(2 * pair + 1)
        when = jnp.where(row < T, first * T + row, second * T + row - T)
        outs = []
        for head in range(2):
            rows = q[:, head * 8 : head * 8 + 8].reshape(2 * T * 8, HD).astype(BF16)
            at = head * 128
            keys = kv_r[:, at : at + 64, :].reshape(NCTX * 64, HD)
            values = kv_r[:, at + 64 : at + 128, :].reshape(NCTX * 64, HD)
            scores = lax.dot_general(
                rows, keys, (((1,), (1,)), ((), ())), preferred_element_type=F32
            )
            scores = jnp.where(when >= seen_from, scores, -1e30)
            top = jnp.max(scores, axis=1, keepdims=True)
            weight = jnp.exp2((scores - top) * factor)
            total = jnp.sum(weight, axis=1, keepdims=True)
            out = jnp.dot(weight.astype(BF16), values, preferred_element_type=F32) / total
            out = jnp.where(when < new_len, out, 0.0)
            outs.append(out.reshape(2 * T, 8, HD))
        both = jnp.concatenate(outs, axis=1).astype(BF16)
        for half in range(2):
            o_s[2 * pair + half] = both[half * T : half * T + T]
            give(1, heads, 2 * pair + half, o_s, att)
        return carry

    lax.fori_loop(0, 4, attend, 0)

    for kind, who, dst in ((0, mine, mix), (1, heads, att)):

        def land_out(giver, carry, kind=kind, who=who, dst=dst):
            own_part = jnp.logical_and(giver == g, who.slot == 0)

            @pl.when(jnp.logical_not(own_part))
            def _():
                place = dst.at[giver]
                remote(
                    {"ctx": who.partner},
                    place,
                    place,
                    out_send.at[kind, giver],
                    out_recv.at[kind, giver],
                ).wait_recv()

            return carry

        lax.fori_loop(0, NREQ, land_out, 0)

    @pl.when(lax.rem(z, 2) == 1)
    def _():
        def sent_edge(o, carry):
            edge_copy(o).wait_send()
            return carry

        lax.fori_loop(0, R, sent_edge, 0)

    for kind, who, src, dst in inputs:

        def sent_in(k, carry, kind=kind, who=who, src=src, dst=dst):
            in_copy(kind, who, lax.rem(who.slot + k, R), src, dst).wait_send()
            return carry

        lax.fori_loop(1, R, sent_in, 0)

    def sent_rest(n, carry):
        pass_copy(n).wait_send()
        for kind, who, src, dst in ((0, mine, y_s, mix), (1, heads, o_s, att)):

            @pl.when(jnp.logical_not(stays(who, n)))
            def _():
                out_copy(kind, who, n, src, dst).wait_send()

        return carry

    lax.fori_loop(0, R, sent_rest, 0)

    def sent_state(i, carry):
        st_copy(i).wait_send()
        return carry

    lax.fori_loop(0, RUNS, sent_state, 0)


def per_device(
    queries,
    kv_pool,
    new_kv,
    block_table,
    cached_len,
    new_len,
    mamba_x,
    conv_state,
    conv_weight,
    conv_bias,
    x_proj,
    dt_raw,
    a_log,
    skip_gain,
    ssm_state,
    target_group,
):
    pool = kv_pool[:, 0].transpose(1, 3, 0, 2, 4).reshape(-1, 2, 2 * PAGE, HD)
    fresh = new_kv.transpose(1, 3, 0, 2, 4)
    vmem = pl.BlockSpec(memory_space=pltpu.VMEM)
    smem = pl.BlockSpec(memory_space=pltpu.SMEM)
    dma = pltpu.SemaphoreType.DMA
    att, mix = pl.pallas_call(
        kernel,
        out_shape=(
            jax.ShapeDtypeStruct((NREQ, T, 16, HD), BF16),
            jax.ShapeDtypeStruct((NREQ, T, C), BF16),
        ),
        in_specs=[vmem] * 12 + [smem] * 4,
        out_specs=(vmem, vmem),
        scratch_shapes=[
            pltpu.VMEM((R, T, C), BF16),
            pltpu.VMEM((R, T, C), BF16),
            pltpu.VMEM((R, T, C), BF16),
            pltpu.VMEM((R, T, C), BF16),
            pltpu.VMEM((R, 256, HD), BF16),
            pltpu.VMEM((R, 256, HD), BF16),
            pltpu.VMEM((R, 256, HD), BF16),
            pltpu.VMEM((2 * R, 256, HD), BF16),
            pltpu.VMEM((3 * TILES, 128), F32),
            pltpu.VMEM((R, 3 * TILES, 128), BF16),
            pltpu.VMEM((RUNS, 3 * TILES, 128), BF16),
            pltpu.VMEM((6 * TILES, 128), F32),
            pltpu.VMEM((S * TILES, 128), F32),
            pltpu.VMEM((RUNS * PAD * TILES, 128), F32),
            pltpu.VMEM((R * T * TILES, 128), F32),
            pltpu.VMEM((R * T * TILES, 128), F32),
            pltpu.VMEM((2 * S, R * T), F32),
            pltpu.VMEM((NTP - 1, 2 * S, R * T), F32),
            pltpu.VMEM((R * T, 2 * S), F32),
            pltpu.VMEM((2 * S * R * T, 128), F32),
            pltpu.VMEM((R * T * S, TILES, 128), F32),
            pltpu.VMEM((R * T * TILES, 128), F32),
            pltpu.VMEM((S * TILES, 128), F32),
            pltpu.VMEM((RUNS, (S + 2) * TILES, 128), BF16),
            pltpu.VMEM((RUNS, (S + 2) * TILES, 128), BF16),
            pltpu.VMEM((R, T, C), BF16),
            pltpu.VMEM((R, T, 16, HD), BF16),
            pltpu.SMEM((NREQ,), jnp.int32),
            dma((4, R)),
            dma((4, R)),
            dma((R,)),
            dma((RUNS,)),
            dma((R,)),
            dma((R,)),
            dma((RUNS,)),
            dma((RUNS,)),
            dma((NTP,)),
            dma((NTP,)),
            dma((2, R)),
            dma((2, NREQ)),
        ],
        compiler_params=pltpu.CompilerParams(
            collective_id=0, has_side_effects=True, vmem_limit_bytes=56 << 20
        ),
    )(
        queries, pool, fresh, mamba_x, dt_raw, conv_weight, conv_bias[None], skip_gain[None],
        a_log, conv_state.transpose(1, 0, 2), x_proj, ssm_state,
        block_table, cached_len[0], new_len[0], target_group[0],
    )
    return att, mix


def solution(mesh):
    in_specs = (
        P("req", "ctx", "tp", None),
        P(None, "req", "ctx", None, "tp", None),
        P(None, "req", "ctx", "tp", None),
        P("req", "ctx", None),
        P("req", None),
        P("req", None),
        P("req", "ctx", "tp"),
        P("req", None, "tp"),
        P(None, "tp"),
        P("tp"),
        P(None, "tp"),
        P("req", "ctx", "tp"),
        P(None, "tp"),
        P("tp"),
        P("req", None, "tp"),
        P("req", None),
    )
    out_specs = (P("req", "ctx", "tp", None), P("req", "ctx", "tp"))
    return jax.shard_map(
        per_device, mesh=mesh, in_specs=in_specs, out_specs=out_specs, check_vma=False
    )
```

time: 673 us -> 163 us (0.24)
  the two profiles are of different devices: /device:TPU:6 before, /device:TPU:1 now
where the time goes in v4:
time: 163 us; the launch traced here: 162 us
  Pallas kernels  155 us (95%)
  local copies, waits for them, and re-layouts  6.1 us (4%)
    pallas_call x1, Pallas kernels, per_device(): pl.pallas_call(kernel, out_shape=(jax.ShapeDtypeStruct((NREQ, T, 16, HD),...  155 us
    unnamed x5, local copies, waits for them, and re-layouts  4.3 us

profile of v4, /device:TPU:1, one launch (start us, length us, event | category | flops | bytes accessed | tf_op | source)
XLA Modules:
  0.0 161.9 jit_solution(8936867099212820877)
XLA Ops:
  0.6 1.6 copy.23
  2.2 1.8 %copy.22 = bf16[48,2,2,8,128]{4,3,2,1,0:T(8,128)(2,1)} copy(bf16[48,2,2,8,128]{4,1,3,0,2:T(2,128)(2,1)} %bitcast.17) | data formatting | bytes 786432 | tf_op jit(solution)/shard_map/transpose | solution.py:526
  4.0 155.2 %shard_map.167 = (bf16[8,16,16,128]{3,2,1,0:T(8,128)(2,1)}, bf16[8,16,2048]{2,1,0:T(8,128)(2,1)}) custom-call(bf16[8,16,16,128]{3,2,1,0:T(8,128)(2,1)} %q_ref.1, bf16[48,2,16,128]{3,2,1,0:T(8,128)(2,1)} %bitcast.15, bf16[8,2,2,16,128]{4,3,2,1,0:T(8,128)(2,1)} %bitcast.16, bf16[8,16,2048]{2,1,0:T(8,128)(2,1)} %x_ref.1, bf16[8,16,2048]{2,1,0:T(8,128)(2,1)} %dt_ref.1, ...), custom_call_target="tpu_custom_call" | custom-call | tf_op jit(solution)/shard_map/pallas_call | solution.py:531
  159.2 0.0 copy-start
  159.2 1.9 %copy.26 = bf16[8,16,16,128]{3,2,1,0:T(8,128)(2,1)} copy(bf16[8,16,16,128]{3,2,1,0:T(8,128)(2,1)} %get-tuple-element.4) | data formatting | bytes 1048576
  161.1 0.0 copy-done
  161.1 0.8 copy.27
Async XLA Ops:
  159.2 1.9 %copy-start = (bf16[8,16,2048]{2,1,0:T(8,128)(2,1)S(1)}, bf16[8,16,2048]{2,1,0:T(8,128)(2,1)}, u32[]{:S(2)}) copy-start(bf16[8,16,2048]{2,1,0:T(8,128)(2,1)} %get-tuple-element.5) | copy-start | bytes 1572868

commit v5 on v4

--- a/solution.py
+++ b/solution.py
@@ -1,3 +1,4 @@
+import functools
 import math
 
 import jax
@@ -115,6 +116,51 @@
         return carry
 
     lax.fori_loop(0, R, fill_scan, 0)
+
+    pl.semaphore_wait(barrier, 2 * (R - 1 + 1 + NREQ) + NTP - 1 + R * lax.rem(z, 2))
+
+    def in_copy(kind, who, slot, src, dst):
+        return remote(
+            {"ctx": who.owner(slot)},
+            src.at[slot],
+            dst.at[who.rank],
+            in_send.at[kind, slot],
+            in_recv.at[kind, who.rank],
+        )
+
+    def in_wait(kind, who, rank, dst):
+        @pl.when(rank != who.rank)
+        def _():
+            place = dst.at[rank]
+            remote(
+                {"ctx": who.partner}, place, place, in_send.at[kind, rank], in_recv.at[kind, rank]
+            ).wait_recv()
+
+    inputs = ((X, mine, x_s, x_r), (KV, heads, kv_s, kv_r), (D, mine, d_s, d_r), (QU, heads, q_s, q_r))
+
+    def edge_copy(slot):
+        return remote(
+            {"ctx": mine.owner(slot, 1 - mine.b)},
+            edge_s.at[slot],
+            edge_r.at[mine.x],
+            edge_send.at[slot],
+            edge_recv.at[mine.x],
+        )
+
+    @pl.when(lax.rem(z, 2) == 1)
+    def _():
+        def send_edge(o, carry):
+            edge_copy(o).start()
+            return carry
+
+        lax.fori_loop(0, R, send_edge, 0)
+
+    def send_in(k, carry, which):
+        for kind, who, src, dst in which:
+            in_copy(kind, who, lax.rem(who.slot + k, R), src, dst).start()
+        return carry
+
+    lax.fori_loop(1, R, functools.partial(send_in, which=inputs[:1]), 0)
 
     def fill_attention(o, carry):
         i = order[o]
@@ -137,52 +183,7 @@
 
     lax.fori_loop(0, R, fill_attention, 0)
 
-    pl.semaphore_wait(barrier, 2 * (R - 1 + 1 + NREQ) + NTP - 1 + R * lax.rem(z, 2))
-
-    def in_copy(kind, who, slot, src, dst):
-        return remote(
-            {"ctx": who.owner(slot)},
-            src.at[slot],
-            dst.at[who.rank],
-            in_send.at[kind, slot],
-            in_recv.at[kind, who.rank],
-        )
-
-    def in_wait(kind, who, rank, dst):
-        @pl.when(rank != who.rank)
-        def _():
-            place = dst.at[rank]
-            remote(
-                {"ctx": who.partner}, place, place, in_send.at[kind, rank], in_recv.at[kind, rank]
-            ).wait_recv()
-
-    inputs = ((X, mine, x_s, x_r), (KV, heads, kv_s, kv_r), (D, mine, d_s, d_r), (QU, heads, q_s, q_r))
-
-    def edge_copy(slot):
-        return remote(
-            {"ctx": mine.owner(slot, 1 - mine.b)},
-            edge_s.at[slot],
-            edge_r.at[mine.x],
-            edge_send.at[slot],
-            edge_recv.at[mine.x],
-        )
-
-    @pl.when(lax.rem(z, 2) == 1)
-    def _():
-        def send_edge(o, carry):
-            edge_copy(o).start()
-            return carry
-
-        lax.fori_loop(0, R, send_edge, 0)
-
-    for pair in (inputs[:2], inputs[2:]):
-
-        def send_pair(k, carry, pair=pair):
-            for kind, who, src, dst in pair:
-                in_copy(kind, who, lax.rem(who.slot + k, R), src, dst).start()
-            return carry
-
-        lax.fori_loop(1, R, send_pair, 0)
+    lax.fori_loop(1, R, functools.partial(send_in, which=inputs[1:2]), 0)
     for kind, who, src, dst in inputs:
         dst[who.rank] = src[who.slot]
 
@@ -223,6 +224,11 @@
         at = ((n // 2) * PAD + 3 + lax.rem(n, 2) * T) * TILES
         for j in range(TILES):
             xf[pl.ds(at + j, T, stride=TILES), :] = rows[:, j * 128 : j * 128 + 128]
+
+        @pl.when(n > 0)
+        def _():
+            send_in(n, 0, inputs[2:])
+
         return carry
 
     lax.fori_loop(0, R, land_x, 0)

time: 163 us -> 168 us (1.031)
  Pallas kernels: 155 us -> 161 us
    pallas_call x1, Pallas kernels: 155 us -> 161 us  [per_device(): pl.pallas_call(kernel, out_shape=(jax.ShapeDtypeStruct((NREQ, T, 16, HD),...]
where the time goes in v5:
time: 168 us
  Pallas kernels  161 us (96%)
  local copies, waits for them, and re-layouts  6.1 us (4%)
    pallas_call x1, Pallas kernels, per_device(): pl.pallas_call(kernel, out_shape=(jax.ShapeDtypeStruct((NREQ, T, 16, HD),...  161 us
    unnamed x5, local copies, waits for them, and re-layouts  4.3 us

profile of v5, /device:TPU:1, one launch (start us, length us, event | category | flops | bytes accessed | tf_op | source)
XLA Modules:
  0.0 168.2 jit_solution(4641647255372125759)
XLA Ops:
  0.6 1.6 copy.23
  2.2 1.8 %copy.22 = bf16[48,2,2,8,128]{4,3,2,1,0:T(8,128)(2,1)} copy(bf16[48,2,2,8,128]{4,1,3,0,2:T(2,128)(2,1)} %bitcast.17) | data formatting | bytes 786432 | tf_op jit(solution)/shard_map/transpose | solution.py:532
  4.0 161.5 %shard_map.167 = (bf16[8,16,16,128]{3,2,1,0:T(8,128)(2,1)}, bf16[8,16,2048]{2,1,0:T(8,128)(2,1)}) custom-call(bf16[8,16,16,128]{3,2,1,0:T(8,128)(2,1)} %q_ref.1, bf16[48,2,16,128]{3,2,1,0:T(8,128)(2,1)} %bitcast.15, bf16[8,2,2,16,128]{4,3,2,1,0:T(8,128)(2,1)} %bitcast.16, bf16[8,16,2048]{2,1,0:T(8,128)(2,1)} %x_ref.1, bf16[8,16,2048]{2,1,0:T(8,128)(2,1)} %dt_ref.1, ...), custom_call_target="tpu_custom_call" | custom-call | tf_op jit(solution)/shard_map/pallas_call | solution.py:537
  165.5 0.0 copy-start
  165.5 1.9 %copy.26 = bf16[8,16,16,128]{3,2,1,0:T(8,128)(2,1)} copy(bf16[8,16,16,128]{3,2,1,0:T(8,128)(2,1)} %get-tuple-element.4) | data formatting | bytes 1048576
  167.4 0.0 copy-done
  167.4 0.8 copy.27
Async XLA Ops:
  165.5 1.9 %copy-start = (bf16[8,16,2048]{2,1,0:T(8,128)(2,1)S(1)}, bf16[8,16,2048]{2,1,0:T(8,128)(2,1)}, u32[]{:S(2)}) copy-start(bf16[8,16,2048]{2,1,0:T(8,128)(2,1)} %get-tuple-element.5) | copy-start | bytes 1572868

commit v6 on v5

--- a/solution.py
+++ b/solution.py
@@ -19,7 +19,7 @@
 SPAN = PAGE * PAGES_REQ
 TILES = C // 128
 RUNS, RUN = 4, 2 * T
-PAD = RUN + 3
+PAD = T + 3
 X, D, KV, QU = range(4)
 
 
@@ -34,7 +34,8 @@
         self.ring = wrap(lax.rem(c, 4) - shift, 4)
         self.b = self.ring // 2
         self.slot = self.x * 2 + self.ring + self.b * (3 - 2 * self.ring)
-        self.rank = self.x * 2 + lax.rem(self.ring, 2)
+        second = lax.rem(self.ring, 2)
+        self.rank = wrap(self.x - shift * self.b * second, 4) * 2 + second
         self.partner = self.x * 4 + lax.rem(3 - self.ring + shift, 4)
 
     def owner(self, slot, b=None):
@@ -44,7 +45,9 @@
 
     def block(self, rank, b=None):
         b = self.b if b is None else b
-        return (rank // 2) * 4 + lax.rem(2 * b + lax.rem(rank, 2) + self.shift, 4)
+        second = lax.rem(rank, 2)
+        x = lax.rem(rank // 2 + self.shift * b * second, 4)
+        return x * 4 + lax.rem(2 * b + second + self.shift, 4)
 
 
 def remote(device, src, dst, send_sem, recv_sem):
@@ -63,27 +66,31 @@
     table, clens, nlens, target,
     att, mix,
     x_s, x_r, d_s, d_r, q_s, q_r, kv_s, kv_r, edge, edge_s, edge_r,
-    taps, a2, xf, xc, dts, pp, pr, pj, sp, av, yl, s0, st_s, st_r, y_s, o_s, order,
+    taps, a2, xf, xc, dts, pp, pr, pj, sp, av, yl, s0, s1, st_s, st_r, y_s, o_s, order,
     in_send, in_recv, edge_send, edge_recv, pass_send, pass_recv, st_send, st_recv,
     tp_send, tp_recv, out_send, out_recv,
 ):
     g, c, p = lax.axis_index("req"), lax.axis_index("ctx"), lax.axis_index("tp")
-    z = lax.rem(c, 4)
-    mine, heads = Owners(c, 0), Owners(c, 1)
+    shift = lax.rem(g, 2)
+    mine, heads = Owners(c, shift), Owners(c, 1 - shift)
+    ends_run = lax.rem(mine.ring, 2)
+    leads = mine.b == shift
+    split = shift * mine.b
 
     barrier = pltpu.get_barrier_semaphore()
 
     def greet(device):
         pl.semaphore_signal(barrier, inc=1, device_id=device, device_id_type=MESH)
 
-    for who in (mine, heads):
+    for kind, who in enumerate((mine, heads)):
 
         def greet_set(k, carry, who=who):
             greet({"ctx": who.owner(lax.rem(who.slot + k, R))})
             return carry
 
-        def greet_givers(k, carry, who=who):
-            greet({"req": k, "ctx": who.owner(wrap(g - k, NREQ))})
+        def greet_givers(k, carry, kind=kind):
+            giver = Owners(c, kind + (1 - 2 * kind) * lax.rem(k, 2))
+            greet({"req": k, "ctx": giver.owner(wrap(g - k, NREQ))})
             return carry
 
         lax.fori_loop(1, R, greet_set, 0)
@@ -92,7 +99,7 @@
     for k in range(1, NTP):
         greet({"tp": wrap(p + k, NTP)})
     for k in range(RUNS):
-        greet({"ctx": k * 4 + 3 - 2 * mine.b})
+        greet({"ctx": mine.block(2 * k + 1, 1 - mine.b)})
 
     for slot in range(NREQ):
         taker = lax.rem(g + slot, NREQ)
@@ -117,7 +124,7 @@
 
     lax.fori_loop(0, R, fill_scan, 0)
 
-    pl.semaphore_wait(barrier, 2 * (R - 1 + 1 + NREQ) + NTP - 1 + R * lax.rem(z, 2))
+    pl.semaphore_wait(barrier, 2 * (R - 1 + 1 + NREQ) + NTP - 1 + R * ends_run)
 
     def in_copy(kind, who, slot, src, dst):
         return remote(
@@ -142,12 +149,12 @@
         return remote(
             {"ctx": mine.owner(slot, 1 - mine.b)},
             edge_s.at[slot],
-            edge_r.at[mine.x],
+            edge_r.at[mine.rank // 2],
             edge_send.at[slot],
-            edge_recv.at[mine.x],
-        )
-
-    @pl.when(lax.rem(z, 2) == 1)
+            edge_recv.at[mine.rank // 2],
+        )
+
+    @pl.when(ends_run == 1)
     def _():
         def send_edge(o, carry):
             edge_copy(o).start()
@@ -183,7 +190,7 @@
 
     lax.fori_loop(0, R, fill_attention, 0)
 
-    lax.fori_loop(1, R, functools.partial(send_in, which=inputs[1:2]), 0)
+    lax.fori_loop(1, R, functools.partial(send_in, which=inputs[1:]), 0)
     for kind, who, src, dst in inputs:
         dst[who.rank] = src[who.slot]
 
@@ -211,30 +218,32 @@
         return carry
 
     lax.fori_loop(0, RUNS, land_edge, 0)
-    leads = mine.b == 0
-    before = edge[...]
+    stored = edge[...]
     for i in range(RUNS):
-        got = edge_r[i].astype(F32)
-        xf[i * PAD * TILES : (i * PAD + 3) * TILES, :] = jnp.where(leads, before, got)
-        before = got
+        late, early = edge_r[i].astype(F32), edge_r[(i + RUNS - 1) % RUNS].astype(F32)
+        if i == 0:
+            early = jnp.where(shift == 0, stored, early)
+        at = 2 * i * PAD * TILES
+        xf[at : at + 3 * TILES, :] = jnp.where(mine.b == 0, early, late)
 
     def land_x(n, carry):
         in_wait(X, mine, n, x_r)
         rows = x_r[n].astype(F32)
-        at = ((n // 2) * PAD + 3 + lax.rem(n, 2) * T) * TILES
+        at = (n * PAD + 3) * TILES
         for j in range(TILES):
             xf[pl.ds(at + j, T, stride=TILES), :] = rows[:, j * 128 : j * 128 + 128]
-
-        @pl.when(n > 0)
-        def _():
-            send_in(n, 0, inputs[2:])
-
         return carry
 
     lax.fori_loop(0, R, land_x, 0)
+    for i in range(RUNS):
+        at = (2 * i + 1) * PAD * TILES
+        rows = xf[at - 3 * TILES : at, :]
+        if i == RUNS - 1:
+            rows = jnp.where(split == 1, stored, rows)
+        xf[at : at + 3 * TILES, :] = rows
 
     def convolve(m, carry):
-        at = (m * 8 + (m // 4) * 3) * TILES
+        at = (m * 8 + (m // 2) * 3) * TILES
         total = jnp.zeros((8, TILES, 128), F32)
         for k in range(4):
             rows = xf[pl.ds(pl.multiple_of(at + k * TILES, TILES), 8 * TILES), :]
@@ -328,7 +337,13 @@
             return (elapsed + d, *new)
 
         zero = jnp.zeros((TILES, 128), F32)
-        last = lax.fori_loop(0, RUN, step, (zero,) * (S + 1))
+
+        def half(h, carry):
+            apart = jnp.logical_and(split == 1, i * 2 + h == 2 * RUNS - 1)
+            carry = tuple(jnp.where(apart, 0.0, v) for v in carry)
+            return lax.fori_loop(h * T, h * T + T, step, carry)
+
+        last = lax.fori_loop(0, 2, half, (zero,) * (S + 1))
         high = last[0].astype(BF16).astype(F32)
         st_s[i] = jnp.concatenate([*last[1:], high, last[0] - high], axis=0).astype(BF16)
         st_copy(i).start()
@@ -359,9 +374,16 @@
 
     own_len = nlens[own]
 
+    def land_state(i, carry):
+        st_copy(i).wait_recv()
+        return carry
+
+    lax.fori_loop(0, RUNS, land_state, 0)
+    s1[...] = s0[...]
+
     def finish_run(i, carry):
-        st_copy(i).wait_recv()
-        own_item, other = st_s[i].astype(F32), st_r[i].astype(F32)
+        own_item = st_s[lax.rem(i + 3 * split, RUNS)].astype(F32)
+        other = st_r[lax.rem(i + 3 * shift * (1 - mine.b), RUNS)].astype(F32)
 
         def advance(item, state):
             elapsed = item[S * TILES : (S + 1) * TILES] + item[(S + 1) * TILES :]
@@ -370,12 +392,17 @@
 
         ahead = s0[...]
         middle = advance(jnp.where(leads, own_item, other), ahead)
-        s0[...] = advance(jnp.where(leads, other, own_item), middle)
-        begin = jnp.where(leads, ahead, middle)
+        after = advance(jnp.where(leads, other, own_item), middle)
+        s0[...] = after
+        begin = jnp.where(split == 1, after, jnp.where(leads, ahead, middle))
 
         def half(h, state):
             rank = i * 2 + h
             first = mine.block(rank) * T
+            apart = jnp.logical_and(split == 1, rank == 2 * RUNS - 1)
+            state = tuple(
+                jnp.where(apart, s1[s * TILES : (s + 1) * TILES, :], state[s]) for s in range(S)
+            )
 
             def step(t, state):
                 at = rank * T + t
@@ -476,7 +503,7 @@
 
         lax.fori_loop(0, NREQ, land_out, 0)
 
-    @pl.when(lax.rem(z, 2) == 1)
+    @pl.when(ends_run == 1)
     def _():
         def sent_edge(o, carry):
             edge_copy(o).wait_send()
@@ -556,7 +583,7 @@
             pltpu.VMEM((RUNS, 3 * TILES, 128), BF16),
             pltpu.VMEM((6 * TILES, 128), F32),
             pltpu.VMEM((S * TILES, 128), F32),
-            pltpu.VMEM((RUNS * PAD * TILES, 128), F32),
+            pltpu.VMEM((R * PAD * TILES, 128), F32),
             pltpu.VMEM((R * T * TILES, 128), F32),
             pltpu.VMEM((R * T * TILES, 128), F32),
             pltpu.VMEM((2 * S, R * T), F32),
@@ -565,6 +592,7 @@
             pltpu.VMEM((2 * S * R * T, 128), F32),
             pltpu.VMEM((R * T * S, TILES, 128), F32),
             pltpu.VMEM((R * T * TILES, 128), F32),
+            pltpu.VMEM((S * TILES, 128), F32),
             pltpu.VMEM((S * TILES, 128), F32),
             pltpu.VMEM((RUNS, (S + 2) * TILES, 128), BF16),
             pltpu.VMEM((RUNS, (S + 2) * TILES, 128), BF16),

time: 168 us -> 161 us (0.958); the launches traced: 168 us -> 159 us
  Pallas kernels: 161 us -> 152 us
    pallas_call x1, Pallas kernels: 161 us -> 152 us  [per_device(): pl.pallas_call(kernel, out_shape=(jax.ShapeDtypeStruct((NREQ, T, 16, HD),...]
where the time goes in v6:
time: 161 us; the launch traced here: 159 us
  Pallas kernels  152 us (94%)
  local copies, waits for them, and re-layouts  6.1 us (4%)
    pallas_call x1, Pallas kernels, per_device(): pl.pallas_call(kernel, out_shape=(jax.ShapeDtypeStruct((NREQ, T, 16, HD),...  152 us
    unnamed x5, local copies, waits for them, and re-layouts  4.3 us

profile of v6, /device:TPU:1, one launch (start us, length us, event | category | flops | bytes accessed | tf_op | source)
XLA Modules:
  0.0 159.0 jit_solution(10192238419939895535)
XLA Ops:
  0.6 1.6 copy.23
  2.2 1.8 %copy.22 = bf16[48,2,2,8,128]{4,3,2,1,0:T(8,128)(2,1)} copy(bf16[48,2,2,8,128]{4,1,3,0,2:T(2,128)(2,1)} %bitcast.17) | data formatting | bytes 786432 | tf_op jit(solution)/shard_map/transpose | solution.py:559
  4.0 152.3 %shard_map.167 = (bf16[8,16,16,128]{3,2,1,0:T(8,128)(2,1)}, bf16[8,16,2048]{2,1,0:T(8,128)(2,1)}) custom-call(bf16[8,16,16,128]{3,2,1,0:T(8,128)(2,1)} %q_ref.1, bf16[48,2,16,128]{3,2,1,0:T(8,128)(2,1)} %bitcast.15, bf16[8,2,2,16,128]{4,3,2,1,0:T(8,128)(2,1)} %bitcast.16, bf16[8,16,2048]{2,1,0:T(8,128)(2,1)} %x_ref.1, bf16[8,16,2048]{2,1,0:T(8,128)(2,1)} %dt_ref.1, ...), custom_call_target="tpu_custom_call" | custom-call | tf_op jit(solution)/shard_map/pallas_call | solution.py:564
  156.3 0.0 copy-start
  156.3 1.9 %copy.26 = bf16[8,16,16,128]{3,2,1,0:T(8,128)(2,1)} copy(bf16[8,16,16,128]{3,2,1,0:T(8,128)(2,1)} %get-tuple-element.4) | data formatting | bytes 1048576
  158.2 0.0 copy-done
  158.2 0.8 copy.27
Async XLA Ops:
  156.3 1.9 %copy-start = (bf16[8,16,2048]{2,1,0:T(8,128)(2,1)S(1)}, bf16[8,16,2048]{2,1,0:T(8,128)(2,1)}, u32[]{:S(2)}) copy-start(bf16[8,16,2048]{2,1,0:T(8,128)(2,1)} %get-tuple-element.5) | copy-start | bytes 1572868

commit v7 on v6

--- a/solution.py
+++ b/solution.py
@@ -190,9 +190,30 @@
 
     lax.fori_loop(0, R, fill_attention, 0)
 
-    lax.fori_loop(1, R, functools.partial(send_in, which=inputs[1:]), 0)
+    lax.fori_loop(1, R, functools.partial(send_in, which=inputs[1:2]), 0)
     for kind, who, src, dst in inputs:
         dst[who.rank] = src[who.slot]
+
+    def pass_copy(n):
+        return remote(
+            {"ctx": heads.partner},
+            kv_r.at[n],
+            kv_r.at[R + n],
+            pass_send.at[n],
+            pass_recv.at[n],
+        )
+
+    def pass_on(n, carry):
+        in_wait(KV, heads, n, kv_r)
+        pass_copy(n).start()
+
+        @pl.when(n > 0)
+        def _():
+            send_in(n, 0, inputs[2:])
+
+        return carry
+
+    lax.fori_loop(0, R, pass_on, 0)
 
     for j in range(TILES):
         lanes = slice(j * 128, j * 128 + 128)
@@ -274,22 +295,6 @@
 
     for k in range(1, NTP):
         tp_copy(k).start()
-
-    def pass_copy(n):
-        return remote(
-            {"ctx": heads.partner},
-            kv_r.at[n],
-            kv_r.at[R + n],
-            pass_send.at[n],
-            pass_recv.at[n],
-        )
-
-    def pass_on(n, carry):
-        in_wait(KV, heads, n, kv_r)
-        pass_copy(n).start()
-        return carry
-
-    lax.fori_loop(0, R, pass_on, 0)
 
     def land_d(n, carry):
         in_wait(D, mine, n, d_r)
@@ -371,66 +376,6 @@
         @pl.when(stays(who, rank))
         def _():
             dst[g] = src[rank]
-
-    own_len = nlens[own]
-
-    def land_state(i, carry):
-        st_copy(i).wait_recv()
-        return carry
-
-    lax.fori_loop(0, RUNS, land_state, 0)
-    s1[...] = s0[...]
-
-    def finish_run(i, carry):
-        own_item = st_s[lax.rem(i + 3 * split, RUNS)].astype(F32)
-        other = st_r[lax.rem(i + 3 * shift * (1 - mine.b), RUNS)].astype(F32)
-
-        def advance(item, state):
-            elapsed = item[S * TILES : (S + 1) * TILES] + item[(S + 1) * TILES :]
-            decay = jnp.exp2(a2[...] * jnp.concatenate([elapsed] * S, axis=0))
-            return decay * state + item[: S * TILES]
-
-        ahead = s0[...]
-        middle = advance(jnp.where(leads, own_item, other), ahead)
-        after = advance(jnp.where(leads, other, own_item), middle)
-        s0[...] = after
-        begin = jnp.where(split == 1, after, jnp.where(leads, ahead, middle))
-
-        def half(h, state):
-            rank = i * 2 + h
-            first = mine.block(rank) * T
-            apart = jnp.logical_and(split == 1, rank == 2 * RUNS - 1)
-            state = tuple(
-                jnp.where(apart, s1[s * TILES : (s + 1) * TILES, :], state[s]) for s in range(S)
-            )
-
-            def step(t, state):
-                at = rank * T + t
-                parts = [yl[position(at), :], None]
-                new = []
-                for s in range(S):
-                    h = av[at * S + s] * state[s]
-                    new.append(h)
-                    y = spread(S + s, at) * h
-                    parts[s % 2] = y if parts[s % 2] is None else parts[s % 2] + y
-                live = jnp.full((TILES, 128), first + t, jnp.int32) < own_len
-                yl[position(at), :] = jnp.where(live, parts[0] + parts[1], 0.0)
-                return tuple(new)
-
-            state = lax.fori_loop(0, T, step, state)
-            rows = [
-                yl[pl.ds(rank * T * TILES + j, T, stride=TILES), :] for j in range(TILES)
-            ]
-            y_s[rank] = jnp.concatenate(rows, axis=1).astype(BF16)
-            give(0, mine, rank, y_s, mix)
-            return state
-
-        lax.fori_loop(
-            0, 2, half, tuple(begin[s * TILES : (s + 1) * TILES] for s in range(S))
-        )
-        return carry
-
-    lax.fori_loop(0, RUNS, finish_run, 0)
 
     def land_kv(n, carry):
         pass_copy(n).wait_recv()
@@ -482,6 +427,66 @@
         return carry
 
     lax.fori_loop(0, 4, attend, 0)
+
+    own_len = nlens[own]
+
+    def land_state(i, carry):
+        st_copy(i).wait_recv()
+        return carry
+
+    lax.fori_loop(0, RUNS, land_state, 0)
+    s1[...] = s0[...]
+
+    def finish_run(i, carry):
+        own_item = st_s[lax.rem(i + 3 * split, RUNS)].astype(F32)
+        other = st_r[lax.rem(i + 3 * shift * (1 - mine.b), RUNS)].astype(F32)
+
+        def advance(item, state):
+            elapsed = item[S * TILES : (S + 1) * TILES] + item[(S + 1) * TILES :]
+            decay = jnp.exp2(a2[...] * jnp.concatenate([elapsed] * S, axis=0))
+            return decay * state + item[: S * TILES]
+
+        ahead = s0[...]
+        middle = advance(jnp.where(leads, own_item, other), ahead)
+        after = advance(jnp.where(leads, other, own_item), middle)
+        s0[...] = after
+        begin = jnp.where(split == 1, after, jnp.where(leads, ahead, middle))
+
+        def half(h, state):
+            rank = i * 2 + h
+            first = mine.block(rank) * T
+            apart = jnp.logical_and(split == 1, rank == 2 * RUNS - 1)
+            state = tuple(
+                jnp.where(apart, s1[s * TILES : (s + 1) * TILES, :], state[s]) for s in range(S)
+            )
+
+            def step(t, state):
+                at = rank * T + t
+                parts = [yl[position(at), :], None]
+                new = []
+                for s in range(S):
+                    h = av[at * S + s] * state[s]
+                    new.append(h)
+                    y = spread(S + s, at) * h
+                    parts[s % 2] = y if parts[s % 2] is None else parts[s % 2] + y
+                live = jnp.full((TILES, 128), first + t, jnp.int32) < own_len
+                yl[position(at), :] = jnp.where(live, parts[0] + parts[1], 0.0)
+                return tuple(new)
+
+            state = lax.fori_loop(0, T, step, state)
+            rows = [
+                yl[pl.ds(rank * T * TILES + j, T, stride=TILES), :] for j in range(TILES)
+            ]
+            y_s[rank] = jnp.concatenate(rows, axis=1).astype(BF16)
+            give(0, mine, rank, y_s, mix)
+            return state
+
+        lax.fori_loop(
+            0, 2, half, tuple(begin[s * TILES : (s + 1) * TILES] for s in range(S))
+        )
+        return carry
+
+    lax.fori_loop(0, RUNS, finish_run, 0)
 
     for kind, who, dst in ((0, mine, mix), (1, heads, att)):
 

time: 161 us -> 159 us (0.988); the launches traced: 159 us -> 159 us
  no operation moved by 1% of the time
where the time goes in v7:
time: 159 us
  Pallas kernels  153 us (96%)
  local copies, waits for them, and re-layouts  6.1 us (4%)
    pallas_call x1, Pallas kernels, per_device(): pl.pallas_call(kernel, out_shape=(jax.ShapeDtypeStruct((NREQ, T, 16, HD),...  153 us
    unnamed x5, local copies, waits for them, and re-layouts  4.3 us

profile of v7, /device:TPU:1, one launch (start us, length us, event | category | flops | bytes accessed | tf_op | source)
XLA Modules:
  0.0 159.2 jit_solution(4292370528289572963)
XLA Ops:
  0.6 1.6 copy.23
  2.2 1.8 %copy.22 = bf16[48,2,2,8,128]{4,3,2,1,0:T(8,128)(2,1)} copy(bf16[48,2,2,8,128]{4,1,3,0,2:T(2,128)(2,1)} %bitcast.17) | data formatting | bytes 786432 | tf_op jit(solution)/shard_map/transpose | solution.py:564
  4.0 152.5 %shard_map.167 = (bf16[8,16,16,128]{3,2,1,0:T(8,128)(2,1)}, bf16[8,16,2048]{2,1,0:T(8,128)(2,1)}) custom-call(bf16[8,16,16,128]{3,2,1,0:T(8,128)(2,1)} %q_ref.1, bf16[48,2,16,128]{3,2,1,0:T(8,128)(2,1)} %bitcast.15, bf16[8,2,2,16,128]{4,3,2,1,0:T(8,128)(2,1)} %bitcast.16, bf16[8,16,2048]{2,1,0:T(8,128)(2,1)} %x_ref.1, bf16[8,16,2048]{2,1,0:T(8,128)(2,1)} %dt_ref.1, ...), custom_call_target="tpu_custom_call" | custom-call | tf_op jit(solution)/shard_map/pallas_call | solution.py:569
  156.5 0.0 copy-start
  156.5 1.9 %copy.26 = bf16[8,16,16,128]{3,2,1,0:T(8,128)(2,1)} copy(bf16[8,16,16,128]{3,2,1,0:T(8,128)(2,1)} %get-tuple-element.4) | data formatting | bytes 1048576
  158.5 0.0 copy-done
  158.5 0.8 copy.27
Async XLA Ops:
  156.5 1.9 %copy-start = (bf16[8,16,2048]{2,1,0:T(8,128)(2,1)S(1)}, bf16[8,16,2048]{2,1,0:T(8,128)(2,1)}, u32[]{:S(2)}) copy-start(bf16[8,16,2048]{2,1,0:T(8,128)(2,1)} %get-tuple-element.5) | copy-start | bytes 1572868

commit v8 on v7

--- a/solution.py
+++ b/solution.py
@@ -23,13 +23,14 @@
 X, D, KV, QU = range(4)
 
 
-def wrap(a, n):
-    return lax.rem(a + n, n)
+def wrap(a, add, n=None):
+    return lax.rem(a + add, add if n is None else n)
 
 
 class Owners:
     def __init__(self, c, shift):
         self.shift = shift
+        self.turn = shift * (NREQ // 2)
         self.x = c // 4
         self.ring = wrap(lax.rem(c, 4) - shift, 4)
         self.b = self.ring // 2
@@ -90,7 +91,7 @@
 
         def greet_givers(k, carry, kind=kind):
             giver = Owners(c, kind + (1 - 2 * kind) * lax.rem(k, 2))
-            greet({"req": k, "ctx": giver.owner(wrap(g - k, NREQ))})
+            greet({"req": k, "ctx": giver.owner(wrap(g - k - giver.turn, 2 * NREQ, NREQ))})
             return carry
 
         lax.fori_loop(1, R, greet_set, 0)
@@ -109,7 +110,7 @@
         order[slot] = found
 
     def fill_scan(o, carry):
-        i = order[o]
+        i = order[lax.rem(o + mine.turn, NREQ)]
         rows = x_ref[i]
         x_s[o] = rows
         d_s[o] = dt_ref[i]
@@ -170,7 +171,7 @@
     lax.fori_loop(1, R, functools.partial(send_in, which=inputs[:1]), 0)
 
     def fill_attention(o, carry):
-        i = order[o]
+        i = order[lax.rem(o + heads.turn, NREQ)]
         q_s[o] = q_ref[i].reshape(2 * T * 8, HD)
         parts = [[[], []], [[], []]]
         for n in range(PAGES_REQ):
@@ -222,7 +223,7 @@
         taps[4 * TILES + j : 4 * TILES + j + 1, :] = bias[0:1, lanes]
         taps[5 * TILES + j : 5 * TILES + j + 1, :] = gains[0:1, lanes]
         a2[pl.ds(j, S, stride=TILES), :] = jnp.exp(a_log[:, lanes]) * (-LOG2E)
-    own = order[mine.slot]
+    own = order[lax.rem(mine.slot + mine.turn, NREQ)]
     old_state = ssm[own].astype(F32)
     for j in range(TILES):
         s0[pl.ds(j, S, stride=TILES), :] = old_state[:, j * 128 : j * 128 + 128]
@@ -358,7 +359,7 @@
 
     def out_copy(kind, who, rank, src, dst):
         return remote(
-            {"req": lax.rem(g + who.slot, NREQ), "ctx": who.block(rank)},
+            {"req": lax.rem(g + who.slot + who.turn, NREQ), "ctx": who.block(rank)},
             src.at[rank],
             dst.at[g],
             out_send.at[kind, rank],
@@ -366,7 +367,7 @@
         )
 
     def stays(who, rank):
-        return jnp.logical_and(who.slot == 0, rank == who.rank)
+        return jnp.logical_and(lax.rem(who.slot + who.turn, NREQ) == 0, rank == who.rank)
 
     def give(kind, who, rank, src, dst):
         @pl.when(jnp.logical_not(stays(who, rank)))
@@ -382,7 +383,7 @@
         return carry
 
     lax.fori_loop(0, R, land_kv, 0)
-    asked = order[heads.slot]
+    asked = order[lax.rem(heads.slot + heads.turn, NREQ)]
     cached_len, new_len = clens[asked], nlens[asked]
     factor = HD**-0.5 * LOG2E
     key = lax.broadcasted_iota(jnp.int32, (1, NCTX * 64), 1)
@@ -491,7 +492,7 @@
     for kind, who, dst in ((0, mine, mix), (1, heads, att)):
 
         def land_out(giver, carry, kind=kind, who=who, dst=dst):
-            own_part = jnp.logical_and(giver == g, who.slot == 0)
+            own_part = jnp.logical_and(giver == g, lax.rem(who.slot + who.turn, NREQ) == 0)
 
             @pl.when(jnp.logical_not(own_part))
             def _():

time: 159 us -> 157 us (0.987)
  the two profiles are of different devices: /device:TPU:1 before, /device:TPU:64 now
where the time goes in v8:
time: 157 us
  Pallas kernels  150 us (96%)
  local copies, waits for them, and re-layouts  6.1 us (4%)
    pallas_call x1, Pallas kernels, per_device(): pl.pallas_call(kernel, out_shape=(jax.ShapeDtypeStruct((NREQ, T, 16, HD),...  150 us
    unnamed x5, local copies, waits for them, and re-layouts  4.3 us

profile of v8, /device:TPU:64, one launch (start us, length us, event | category | flops | bytes accessed | tf_op | source)
XLA Modules:
  0.0 157.0 jit_solution(7557989866472127188)
XLA Ops:
  0.6 1.6 %copy.23 = bf16[2,8,16,2,128]{4,2,0,3,1:T(8,128)(2,1)} copy(bf16[2,8,16,2,128]{4,3,2,1,0:T(2,128)(2,1)} %param.18) | data formatting | bytes 262144 | tf_op args[2]
  2.2 1.8 %copy.22 = bf16[48,2,2,8,128]{4,3,2,1,0:T(8,128)(2,1)} copy(bf16[48,2,2,8,128]{4,1,3,0,2:T(2,128)(2,1)} %bitcast.17) | data formatting | bytes 786432 | tf_op jit(solution)/shard_map/transpose | solution.py:565
  4.0 150.2 %shard_map.167 = (bf16[8,16,16,128]{3,2,1,0:T(8,128)(2,1)}, bf16[8,16,2048]{2,1,0:T(8,128)(2,1)}) custom-call(bf16[8,16,16,128]{3,2,1,0:T(8,128)(2,1)} %q_ref.1, bf16[48,2,16,128]{3,2,1,0:T(8,128)(2,1)} %bitcast.15, bf16[8,2,2,16,128]{4,3,2,1,0:T(8,128)(2,1)} %bitcast.16, bf16[8,16,2048]{2,1,0:T(8,128)(2,1)} %x_ref.1, bf16[8,16,2048]{2,1,0:T(8,128)(2,1)} %dt_ref.1, ...), custom_call_target="tpu_custom_call" | custom-call | tf_op jit(solution)/shard_map/pallas_call | solution.py:570
  154.2 0.0 copy-start
  154.2 1.9 %copy.26 = bf16[8,16,16,128]{3,2,1,0:T(8,128)(2,1)} copy(bf16[8,16,16,128]{3,2,1,0:T(8,128)(2,1)} %get-tuple-element.4) | data formatting | bytes 1048576
  156.2 0.0 copy-done
  156.2 0.8 copy.27
Async XLA Ops:
  154.2 1.9 %copy-start = (bf16[8,16,2048]{2,1,0:T(8,128)(2,1)S(1)}, bf16[8,16,2048]{2,1,0:T(8,128)(2,1)}, u32[]{:S(2)}) copy-start(bf16[8,16,2048]{2,1,0:T(8,128)(2,1)} %get-tuple-element.5) | copy-start | bytes 1572868

commit v9 on v8

--- a/solution.py
+++ b/solution.py
@@ -144,7 +144,7 @@
                 {"ctx": who.partner}, place, place, in_send.at[kind, rank], in_recv.at[kind, rank]
             ).wait_recv()
 
-    inputs = ((X, mine, x_s, x_r), (KV, heads, kv_s, kv_r), (D, mine, d_s, d_r), (QU, heads, q_s, q_r))
+    inputs = ((X, mine, x_s, x_r), (D, mine, d_s, d_r), (KV, heads, kv_s, kv_r), (QU, heads, q_s, q_r))
 
     def edge_copy(slot):
         return remote(
@@ -168,7 +168,7 @@
             in_copy(kind, who, lax.rem(who.slot + k, R), src, dst).start()
         return carry
 
-    lax.fori_loop(1, R, functools.partial(send_in, which=inputs[:1]), 0)
+    lax.fori_loop(1, R, functools.partial(send_in, which=inputs[:2]), 0)
 
     def fill_attention(o, carry):
         i = order[lax.rem(o + heads.turn, NREQ)]
@@ -191,7 +191,7 @@
 
     lax.fori_loop(0, R, fill_attention, 0)
 
-    lax.fori_loop(1, R, functools.partial(send_in, which=inputs[1:2]), 0)
+    lax.fori_loop(1, R, functools.partial(send_in, which=inputs[2:3]), 0)
     for kind, who, src, dst in inputs:
         dst[who.rank] = src[who.slot]
 
@@ -210,7 +210,7 @@
 
         @pl.when(n > 0)
         def _():
-            send_in(n, 0, inputs[2:])
+            send_in(n, 0, inputs[3:])
 
         return carry
 

time: 157 us -> 151 us (0.962)
  the two profiles are of different devices: /device:TPU:64 before, /device:TPU:88 now
where the time goes in v9:
time: 151 us
  Pallas kernels  144 us (95%)
  local copies, waits for them, and re-layouts  6.1 us (4%)
    pallas_call x1, Pallas kernels, per_device(): pl.pallas_call(kernel, out_shape=(jax.ShapeDtypeStruct((NREQ, T, 16, HD),...  144 us
    unnamed x5, local copies, waits for them, and re-layouts  4.3 us

profile of v9, /device:TPU:88, one launch (start us, length us, event | category | flops | bytes accessed | tf_op | source)
XLA Modules:
  0.0 150.8 jit_solution(2701484631426753927)
XLA Ops:
  0.6 1.6 %copy.23 = bf16[2,8,16,2,128]{4,2,0,3,1:T(8,128)(2,1)} copy(bf16[2,8,16,2,128]{4,3,2,1,0:T(2,128)(2,1)} %param.18) | data formatting | bytes 262144 | tf_op args[2]
  2.2 1.8 %copy.22 = bf16[48,2,2,8,128]{4,3,2,1,0:T(8,128)(2,1)} copy(bf16[48,2,2,8,128]{4,1,3,0,2:T(2,128)(2,1)} %bitcast.17) | data formatting | bytes 786432 | tf_op jit(solution)/shard_map/transpose | solution.py:565
  4.0 144.1 %shard_map.167 = (bf16[8,16,16,128]{3,2,1,0:T(8,128)(2,1)}, bf16[8,16,2048]{2,1,0:T(8,128)(2,1)}) custom-call(bf16[8,16,16,128]{3,2,1,0:T(8,128)(2,1)} %q_ref.1, bf16[48,2,16,128]{3,2,1,0:T(8,128)(2,1)} %bitcast.15, bf16[8,2,2,16,128]{4,3,2,1,0:T(8,128)(2,1)} %bitcast.16, bf16[8,16,2048]{2,1,0:T(8,128)(2,1)} %x_ref.1, bf16[8,16,2048]{2,1,0:T(8,128)(2,1)} %dt_ref.1, ...), custom_call_target="tpu_custom_call" | custom-call | tf_op jit(solution)/shard_map/pallas_call | solution.py:570
  148.1 0.0 copy-start
  148.1 1.9 %copy.26 = bf16[8,16,16,128]{3,2,1,0:T(8,128)(2,1)} copy(bf16[8,16,16,128]{3,2,1,0:T(8,128)(2,1)} %get-tuple-element.4) | data formatting | bytes 1048576
  150.0 0.0 copy-done
  150.0 0.8 copy.27
Async XLA Ops:
  148.1 1.9 %copy-start = (bf16[8,16,2048]{2,1,0:T(8,128)(2,1)S(1)}, bf16[8,16,2048]{2,1,0:T(8,128)(2,1)}, u32[]{:S(2)}) copy-start(bf16[8,16,2048]{2,1,0:T(8,128)(2,1)} %get-tuple-element.5) | copy-start | bytes 1572868
